TPU v7x, 32 devices: a whole 2x2x4 slice. The times are simulated.
32 devices in a mesh: dp: 16 (over z, x, core), fsdp: 2 (over y).
Axes of the slice: x: 2, y: 2, z: 4, core: 2. Of those that a mesh axis runs over, the one named last changes fastest.
Arguments:
- tokens: bfloat16 [32768, 768], P(('dp', 'fsdp')), may hold values from -8 to 8
- segment_ids: int32 [64, 512], P(('dp', 'fsdp')), may hold values from 0 to 3, never falling along the last dimension, each value on 1 to 256 neighbouring positions
- valid: int32 [64, 512], P(('dp', 'fsdp')), may hold values from 0 to 1, as said below
- input_weight: bfloat16 [768, 2304], P(('dp', 'fsdp')), may hold values from -0.21875 to 0.21875
- query_bias: bfloat16 [768], P(('dp', 'fsdp')), may hold values from -3 to 3
- value_bias: bfloat16 [768], P(('dp', 'fsdp')), may hold values from -3 to 3
- output_weight: bfloat16 [768, 768], P(('dp', 'fsdp')), may hold values from -1.25 to 1.25
- output_bias: bfloat16 [768], P(('dp', 'fsdp')), may hold values from -3 to 3
- first_gain: bfloat16 [768], P(('dp', 'fsdp')), may hold values from 0.099609375 to 1.8984375
- first_shift: bfloat16 [768], P(('dp', 'fsdp')), may hold values from -3 to 3
- expand_weight: bfloat16 [768, 3072], P(('dp', 'fsdp')), may hold values from -0.21875 to 0.21875
- expand_bias: bfloat16 [3072], P(('dp', 'fsdp')), may hold values from -3 to 3
- shrink_weight: bfloat16 [3072, 768], P(('dp', 'fsdp')), may hold values from -0.15625 to 0.15625
- shrink_bias: bfloat16 [768], P(('dp', 'fsdp')), may hold values from -3 to 3
- second_gain: bfloat16 [768], P(('dp', 'fsdp')), may hold values from 0.099609375 to 1.8984375
- second_shift: bfloat16 [768], P(('dp', 'fsdp')), may hold values from -3 to 3
- cotangent: bfloat16 [32768, 768], P(('dp', 'fsdp')), may hold values from -6 to 6
Outputs:
- layer_output: bfloat16 [32768, 768], P(('dp', 'fsdp'))
- token_gradient: float32 [32768, 768], P(('dp', 'fsdp'))
- statistics: float32 [4], replicated
- input_weight_gradient: float32 [768, 2304], P(('dp', 'fsdp'))
- query_bias_gradient: float32 [768], P(('dp', 'fsdp'))
- value_bias_gradient: float32 [768], P(('dp', 'fsdp'))
- output_weight_gradient: float32 [768, 768], P(('dp', 'fsdp'))
- output_bias_gradient: float32 [768], P(('dp', 'fsdp'))
- first_gain_gradient: float32 [768], P(('dp', 'fsdp'))
- first_shift_gradient: float32 [768], P(('dp', 'fsdp'))
- expand_weight_gradient: float32 [768, 3072], P(('dp', 'fsdp'))
- expand_bias_gradient: float32 [3072], P(('dp', 'fsdp'))
- shrink_weight_gradient: float32 [3072, 768], P(('dp', 'fsdp'))
- shrink_bias_gradient: float32 [768], P(('dp', 'fsdp'))
- second_gain_gradient: float32 [768], P(('dp', 'fsdp'))
- second_shift_gradient: float32 [768], P(('dp', 'fsdp'))
Inputs may be any that keep to these rules, and one draw needn't show every extreme that they name: 1 marks a valid token; the first token of every sequence is valid.
All inputs are finite; a program needn't handle non-finite values.
Results may differ from a plain program's by a relative error of at most 0.014.
Values may be sent and summed in bfloat16 or wider, within the bound.
A program may use at most 192 MiB of HBM per device.

v0:
```python
import jax
import jax.numpy as jnp
from jax import lax
from jax.sharding import PartitionSpec as P

HEAD_DIM = 64


def layer_norm(value, gain, shift):
    centred = value - jnp.mean(value, axis=-1, keepdims=True)
    spread = jnp.mean(centred * centred, axis=-1, keepdims=True)
    return centred * lax.rsqrt(spread + 1e-12) * gain + shift


def gelu_exact(value):
    return 0.5 * value * (1.0 + lax.erf(value * 0.7071067811865476))


def attention_mask(segment_ids, valid):
    length = segment_ids.shape[1]
    same_doc = segment_ids[:, :, None] == segment_ids[:, None, :]
    diagonal = jnp.arange(length)[:, None] == jnp.arange(length)[None, :]
    return same_doc & ((valid[:, None, :] > 0) | diagonal[None])


def head_scores(queries, key_rows, allowed):
    raw_scores = jnp.einsum(
        "sqhe,skhe->shqk", queries, key_rows, preferred_element_type=jnp.float32
    ) * HEAD_DIM ** (-0.5)
    return jnp.where(allowed[:, None], raw_scores, -1e30)


def forward_pass(params, tokens, segment_ids, valid):
    (
        input_weight,
        query_bias,
        value_bias,
        output_weight,
        output_bias,
        first_gain,
        first_shift,
        expand_weight,
        expand_bias,
        shrink_weight,
        shrink_bias,
        second_gain,
        second_shift,
    ) = params
    sequences, length = segment_ids.shape
    features = tokens.shape[1]
    heads = features // HEAD_DIM
    shape_four = (sequences, length, heads, HEAD_DIM)
    combined = jnp.dot(tokens, input_weight, preferred_element_type=jnp.float32)
    queries = (
        (combined[:, :features] + query_bias.astype(jnp.float32))
        .astype(jnp.bfloat16)
        .reshape(shape_four)
    )
    key_rows = combined[:, features : 2 * features].astype(jnp.bfloat16).reshape(shape_four)
    value_rows = (
        (combined[:, 2 * features :] + value_bias.astype(jnp.float32))
        .astype(jnp.bfloat16)
        .reshape(shape_four)
    )
    allowed = attention_mask(segment_ids, valid)
    scores = head_scores(queries, key_rows, allowed)
    highest_score = jnp.max(scores, axis=-1, keepdims=True)
    exponent = jnp.exp(scores - highest_score)
    row_totals = jnp.sum(exponent, axis=-1, keepdims=True)
    log_total = highest_score + jnp.log(row_totals)
    weights_low = (exponent / row_totals).astype(jnp.bfloat16)
    attended = jnp.einsum(
        "shqk,skhe->sqhe", weights_low, value_rows, preferred_element_type=jnp.float32
    )
    attended = attended.astype(jnp.bfloat16).reshape(sequences * length, features)
    branch = jnp.dot(
        attended, output_weight, preferred_element_type=jnp.float32
    ) + output_bias.astype(jnp.float32)
    residual = tokens.astype(jnp.float32) + branch
    normed = layer_norm(
        residual, first_gain.astype(jnp.float32), first_shift.astype(jnp.float32)
    ).astype(jnp.bfloat16)
    hidden_pre = jnp.dot(
        normed, expand_weight, preferred_element_type=jnp.float32
    ) + expand_bias.astype(jnp.float32)
    activated = gelu_exact(hidden_pre).astype(jnp.bfloat16)
    feedfwd = jnp.dot(
        activated, shrink_weight, preferred_element_type=jnp.float32
    ) + shrink_bias.astype(jnp.float32)
    second = normed.astype(jnp.float32) + feedfwd
    result = layer_norm(second, second_gain.astype(jnp.float32), second_shift.astype(jnp.float32))
    counted = valid.reshape(-1).astype(jnp.float32)
    stat_sums = jnp.stack(
        [
            jnp.sum(
                counted
                * jnp.sum(jnp.square(member.astype(jnp.bfloat16).astype(jnp.float32)), axis=-1)
            )
            for member in (residual, branch, second, feedfwd)
        ]
    )
    stored = (
        queries,
        key_rows,
        value_rows,
        allowed,
        log_total,
        attended,
        residual,
        normed,
        hidden_pre,
        activated,
        second,
    )
    return (result, stat_sums, stored)


def backward_pass(params, tokens, stored, cotangent):
    (
        input_weight,
        query_bias,
        value_bias,
        output_weight,
        output_bias,
        first_gain,
        first_shift,
        expand_weight,
        expand_bias,
        shrink_weight,
        shrink_bias,
        second_gain,
        second_shift,
    ) = params
    (
        queries,
        key_rows,
        value_rows,
        allowed,
        log_total,
        attended,
        residual,
        normed,
        hidden_pre,
        activated,
        second,
    ) = stored
    features = tokens.shape[1]
    flat_shape = (tokens.shape[0], features)
    scale = HEAD_DIM ** (-0.5)
    second_value, second_pull = jax.vjp(
        layer_norm, second, second_gain.astype(jnp.float32), second_shift.astype(jnp.float32)
    )
    second_grad, second_gain_grad, second_shift_grad = second_pull(cotangent.astype(jnp.float32))
    feedfwd_grad = second_grad.astype(jnp.bfloat16)
    shrink_bias_grad = jnp.sum(feedfwd_grad, axis=0, dtype=jnp.float32)
    shrink_weight_grad = jnp.dot(activated.T, feedfwd_grad, preferred_element_type=jnp.float32)
    activated_grad = jnp.dot(feedfwd_grad, shrink_weight.T, preferred_element_type=jnp.float32)
    gelu_value, gelu_pull = jax.vjp(gelu_exact, hidden_pre)
    hidden_grad = gelu_pull(activated_grad)[0].astype(jnp.bfloat16)
    expand_bias_grad = jnp.sum(hidden_grad, axis=0, dtype=jnp.float32)
    expand_weight_grad = jnp.dot(normed.T, hidden_grad, preferred_element_type=jnp.float32)
    normed_grad = second_grad + jnp.dot(
        hidden_grad, expand_weight.T, preferred_element_type=jnp.float32
    )
    first_value, first_pull = jax.vjp(
        layer_norm, residual, first_gain.astype(jnp.float32), first_shift.astype(jnp.float32)
    )
    residual_grad, first_gain_grad, first_shift_grad = first_pull(normed_grad)
    branch_grad = residual_grad.astype(jnp.bfloat16)
    output_bias_grad = jnp.sum(branch_grad, axis=0, dtype=jnp.float32)
    output_weight_grad = jnp.dot(attended.T, branch_grad, preferred_element_type=jnp.float32)
    attended_grad = jnp.dot(branch_grad, output_weight.T, preferred_element_type=jnp.float32)
    attended_grad = attended_grad.astype(jnp.bfloat16).reshape(queries.shape)
    scores = head_scores(queries, key_rows, allowed)
    probabilities = jnp.exp(scores - log_total)
    weights_low = probabilities.astype(jnp.bfloat16)
    prob_grad = jnp.einsum(
        "sqhe,skhe->shqk", attended_grad, value_rows, preferred_element_type=jnp.float32
    )
    value_grad = jnp.einsum(
        "shqk,sqhe->skhe", weights_low, attended_grad, preferred_element_type=jnp.float32
    ).astype(jnp.bfloat16)
    inner = jnp.sum(probabilities * prob_grad, axis=-1, keepdims=True)
    score_grad = (probabilities * (prob_grad - inner)).astype(jnp.bfloat16)
    query_grad = (
        jnp.einsum("shqk,skhe->sqhe", score_grad, key_rows, preferred_element_type=jnp.float32)
        * scale
    ).astype(jnp.bfloat16)
    key_grad = (
        jnp.einsum("shqk,sqhe->skhe", score_grad, queries, preferred_element_type=jnp.float32)
        * scale
    ).astype(jnp.bfloat16)
    query_flat = query_grad.reshape(flat_shape)
    value_flat = value_grad.reshape(flat_shape)
    combined_grad = jnp.concatenate([query_flat, key_grad.reshape(flat_shape), value_flat], axis=1)
    query_bias_grad = jnp.sum(query_flat, axis=0, dtype=jnp.float32)
    value_bias_grad = jnp.sum(value_flat, axis=0, dtype=jnp.float32)
    input_weight_grad = jnp.dot(tokens.T, combined_grad, preferred_element_type=jnp.float32)
    token_grad = residual_grad + jnp.dot(
        combined_grad, input_weight.T, preferred_element_type=jnp.float32
    )
    gradients = (
        input_weight_grad,
        query_bias_grad,
        value_bias_grad,
        output_weight_grad,
        output_bias_grad,
        first_gain_grad,
        first_shift_grad,
        expand_weight_grad,
        expand_bias_grad,
        shrink_weight_grad,
        shrink_bias_grad,
        second_gain_grad,
        second_shift_grad,
    )
    return (token_grad, gradients)


def per_device(
    tokens,
    segment_ids,
    valid,
    input_weight,
    query_bias,
    value_bias,
    output_weight,
    output_bias,
    first_gain,
    first_shift,
    expand_weight,
    expand_bias,
    shrink_weight,
    shrink_bias,
    second_gain,
    second_shift,
    cotangent,
):
    shards = (
        input_weight,
        query_bias,
        value_bias,
        output_weight,
        output_bias,
        first_gain,
        first_shift,
        expand_weight,
        expand_bias,
        shrink_weight,
        shrink_bias,
        second_gain,
        second_shift,
    )
    params = (
        lax.all_gather(shards[0], ("dp", "fsdp"), axis=0, tiled=True),
        lax.all_gather(shards[1], ("dp", "fsdp"), axis=0, tiled=True),
        lax.all_gather(shards[2], ("dp", "fsdp"), axis=0, tiled=True),
        lax.all_gather(shards[3], ("dp", "fsdp"), axis=0, tiled=True),
        lax.all_gather(shards[4], ("dp", "fsdp"), axis=0, tiled=True),
        lax.all_gather(shards[5], ("dp", "fsdp"), axis=0, tiled=True),
        lax.all_gather(shards[6], ("dp", "fsdp"), axis=0, tiled=True),
        lax.all_gather(shards[7], ("dp", "fsdp"), axis=0, tiled=True),
        lax.all_gather(shards[8], ("dp", "fsdp"), axis=0, tiled=True),
        lax.all_gather(shards[9], ("dp", "fsdp"), axis=0, tiled=True),
        lax.all_gather(shards[10], ("dp", "fsdp"), axis=0, tiled=True),
        lax.all_gather(shards[11], ("dp", "fsdp"), axis=0, tiled=True),
        lax.all_gather(shards[12], ("dp", "fsdp"), axis=0, tiled=True),
    )
    result, stat_sums, stored = forward_pass(params, tokens, segment_ids, valid)
    local_count = jnp.sum(valid, dtype=jnp.float32)
    total_sums, total_count = lax.psum((stat_sums, local_count), ("dp", "fsdp"))
    statistics = total_sums / (tokens.shape[1] * total_count)
    params = (
        lax.all_gather(shards[0], ("dp", "fsdp"), axis=0, tiled=True),
        lax.all_gather(shards[1], ("dp", "fsdp"), axis=0, tiled=True),
        lax.all_gather(shards[2], ("dp", "fsdp"), axis=0, tiled=True),
        lax.all_gather(shards[3], ("dp", "fsdp"), axis=0, tiled=True),
        lax.all_gather(shards[4], ("dp", "fsdp"), axis=0, tiled=True),
        lax.all_gather(shards[5], ("dp", "fsdp"), axis=0, tiled=True),
        lax.all_gather(shards[6], ("dp", "fsdp"), axis=0, tiled=True),
        lax.all_gather(shards[7], ("dp", "fsdp"), axis=0, tiled=True),
        lax.all_gather(shards[8], ("dp", "fsdp"), axis=0, tiled=True),
        lax.all_gather(shards[9], ("dp", "fsdp"), axis=0, tiled=True),
        lax.all_gather(shards[10], ("dp", "fsdp"), axis=0, tiled=True),
        lax.all_gather(shards[11], ("dp", "fsdp"), axis=0, tiled=True),
        lax.all_gather(shards[12], ("dp", "fsdp"), axis=0, tiled=True),
    )
    unused_result, unused_sums, stored = forward_pass(params, tokens, segment_ids, valid)
    token_grad, gradients = backward_pass(params, tokens, stored, cotangent)
    owned = (
        lax.psum_scatter(gradients[0], ("dp", "fsdp"), scatter_dimension=0, tiled=True),
        lax.psum_scatter(gradients[1], ("dp", "fsdp"), scatter_dimension=0, tiled=True),
        lax.psum_scatter(gradients[2], ("dp", "fsdp"), scatter_dimension=0, tiled=True),
        lax.psum_scatter(gradients[3], ("dp", "fsdp"), scatter_dimension=0, tiled=True),
        lax.psum_scatter(gradients[4], ("dp", "fsdp"), scatter_dimension=0, tiled=True),
        lax.psum_scatter(gradients[5], ("dp", "fsdp"), scatter_dimension=0, tiled=True),
        lax.psum_scatter(gradients[6], ("dp", "fsdp"), scatter_dimension=0, tiled=True),
        lax.psum_scatter(gradients[7], ("dp", "fsdp"), scatter_dimension=0, tiled=True),
        lax.psum_scatter(gradients[8], ("dp", "fsdp"), scatter_dimension=0, tiled=True),
        lax.psum_scatter(gradients[9], ("dp", "fsdp"), scatter_dimension=0, tiled=True),
        lax.psum_scatter(gradients[10], ("dp", "fsdp"), scatter_dimension=0, tiled=True),
        lax.psum_scatter(gradients[11], ("dp", "fsdp"), scatter_dimension=0, tiled=True),
        lax.psum_scatter(gradients[12], ("dp", "fsdp"), scatter_dimension=0, tiled=True),
    )
    return (
        result.astype(jnp.bfloat16),
        token_grad,
        statistics,
        owned[0],
        owned[1],
        owned[2],
        owned[3],
        owned[4],
        owned[5],
        owned[6],
        owned[7],
        owned[8],
        owned[9],
        owned[10],
        owned[11],
        owned[12],
    )


def solution(mesh):
    in_specs = (
        P(("dp", "fsdp"), None),
        P(("dp", "fsdp"), None),
        P(("dp", "fsdp"), None),
        P(("dp", "fsdp"), None),
        P(("dp", "fsdp")),
        P(("dp", "fsdp")),
        P(("dp", "fsdp"), None),
        P(("dp", "fsdp")),
        P(("dp", "fsdp")),
        P(("dp", "fsdp")),
        P(("dp", "fsdp"), None),
        P(("dp", "fsdp")),
        P(("dp", "fsdp"), None),
        P(("dp", "fsdp")),
        P(("dp", "fsdp")),
        P(("dp", "fsdp")),
        P(("dp", "fsdp"), None),
    )
    out_specs = (
        P(("dp", "fsdp"), None),
        P(("dp", "fsdp"), None),
        P(),
        P(("dp", "fsdp"), None),
        P(("dp", "fsdp")),
        P(("dp", "fsdp")),
        P(("dp", "fsdp"), None),
        P(("dp", "fsdp")),
        P(("dp", "fsdp")),
        P(("dp", "fsdp")),
        P(("dp", "fsdp"), None),
        P(("dp", "fsdp")),
        P(("dp", "fsdp"), None),
        P(("dp", "fsdp")),
        P(("dp", "fsdp")),
        P(("dp", "fsdp")),
    )
    return jax.shard_map(
        per_device, mesh=mesh, in_specs=in_specs, out_specs=out_specs, check_vma=False
    )
```

profile of v0, /device:TPU:0, one launch (start us, length us, event | category | flops | bytes accessed | tf_op | source)
XLA Modules:
  0.0 828.5 jit_solution(14291311724258726516)
XLA Ops:
  18.4 42.5 %all-reduce.19 = (bf16[768]{0:T(1024)(128)(2,1)S(1)}, bf16[768]{0:T(1024)(128)(2,1)S(1)}, bf16[768]{0:T(1024)(128)(2,1)S(1)}, bf16[768]{0:T(1024)(128)(2,1)S(1)}...) all-reduce(bf16[768]{0:T(1024)(128)(2,1)S(1)} %dynamic-update-slice, ...), channel_id=1, replica_groups=mesh['dp'=16,'fsdp'=2] {'dp','fsdp'}, use_global_device_ids=true, to_apply=%add.1 | all-reduce | flops 9216 | bytes 36864
  65.6 8.4 %all-gather.5.cloned.1.call-done = bf16[768,2304]{1,0:T(8,128)(2,1)} async-done(((bf16[24,2304]{1,0:T(8,128)(2,1)}), bf16[768,2304]{1,0:T(8,128)(2,1)}) %all-gather.5.cloned.1.call-update) | async-done | bytes 3538960 | tf_op jit(solution)/shard_map/all_gather | solution.py:255
  74.1 5.8 fusion.44
  79.9 3.6 copy-done.9
  88.2 5.7 fusion.12
  96.5 3.8 reshape.167
  100.3 12.0 %fusion.6 = (f32[2,12,512]{2,1,0:T(8,128)S(1)}, f32[2,12,512,512]{2,3,1,0:T(8,128)}) fusion(pred[2,512,512]{1,2,0:T(8,128)(4,1)} %or_and_fusion, bf16[2,512,12,64]{1,0,3,2:T(2,128)(2,1)S(1)} %reshape.168, bf16[2,512,12,64]{1,0,3,2:T(2,128)(2,1)} %reshape.167), kind=kOutput, calls=%fused_computation.15 | convolution fusion | flops 824168448 | bytes 28884992 | tf_op jit(solution)/shard_map/sqhe,skhe->shqk/dot_general | solution.py:27
  115.0 3.9 reshape.166
  118.9 11.2 %fusion = f32[2,12,512]{2,1,0:T(8,128)S(1)} fusion(f32[2,12,512]{2,1,0:T(8,128)S(1)} %get-tuple-element.116, f32[2,12,512,512]{2,3,1,0:T(8,128)} %get-tuple-element.117, pred[2,512,512]{1,2,0:T(8,128)(4,1)S(1)} %copy-done.3), kind=kLoop, calls=%fused_computation.6 | loop fusion | flops 25153536 | bytes 25788416 | tf_op jit(solution)/shard_map/reduce_sum | solution.py:69
  130.1 11.9 %fusion.22 = bf16[2,512,12,64]{1,3,2,0:T(8,128)(2,1)S(1)} fusion(f32[2,12,512]{2,1,0:T(8,128)S(1)} %fusion, f32[2,12,512]{2,1,0:T(8,128)S(1)} %get-tuple-element.116, f32[2,12,512,512]{2,3,1,0:T(8,128)} %get-tuple-element.117, pred[2,512,512]{1,2,0:T(8,128)(4,1)S(1)} %copy-done.3, bf16[2,512,12,64]{1,0,3,2:T(2,128)(2,1)S(1)} %copy-done.10), kind=kOutput, calls=%fused_computation.62 | convolution fusion | flops 837550080 | bytes 28934144 | tf_op jit(solution)/shard_map/shqk,skhe->sqhe/dot_general | solution.py:72
  145.2 4.7 fusion.42
  152.0 43.5 %all-gather.9.cloned.1.call-done = bf16[768,3072]{1,0:T(8,128)(2,1)} async-done(((bf16[24,3072]{1,0:T(8,128)(2,1)}), bf16[768,3072]{1,0:T(8,128)(2,1)}) %all-gather.9.cloned.1.call-update) | async-done | bytes 4718608 | tf_op jit(solution)/shard_map/all_gather | solution.py:262
  195.4 13.5 %multiply_convert_fusion.1 = (bf16[1024,3072]{1,0:T(8,128)(2,1)}, f32[1024,3072]{1,0:T(8,128)}) fusion(f32[3072]{0:T(1024)S(1)} %convert_element_type.177, bf16[768,3072]{1,0:T(8,128)(2,1)} %all-gather.9.cloned.1.call-done, f32[1024,768]{0,1:T(8,128)} %copy-done.6, f32[768]{0:T(1024)S(1)} %convert_element_type.174, f32[768]{0:T(1024)S(1)} %convert_element_type.173, ...), kind=kOutput, calls=%fused_computation.12 | convolution fusion | flops 4854644736 | bytes 26765312 | tf_op jit(solution)/shard_map/dot_general | solution.py:83
  209.0 51.7 %all-gather.11.cloned.1.call-done = bf16[3072,768]{1,0:T(8,128)(2,1)} async-done(((bf16[96,768]{1,0:T(8,128)(2,1)}), bf16[3072,768]{1,0:T(8,128)(2,1)}) %all-gather.11.cloned.1.call-update) | async-done | bytes 4718608 | tf_op jit(solution)/shard_map/all_gather | solution.py:264
  260.7 9.9 %fusion.41 = (f32[1024]{0:T(1024)S(1)}, f32[1024,768]{0,1:T(8,128)S(1)}, f32[1024]{0:T(1024)S(1)}) fusion(f32[768]{0:T(1024)S(1)} %convert_element_type.179, bf16[1024,3072]{1,0:T(8,128)(2,1)} %get-tuple-element.118, bf16[3072,768]{1,0:T(8,128)(2,1)} %all-gather.11.cloned.1.call-done, f32[768]{0:T(1024)S(1)} %convert_element_type.174, ...), kind=kOutput, calls=%fused_computation.102 | convolution fusion | flops 4842059776 | bytes 17327104 | tf_op jit(solution)/shard_map/dot_general | solution.py:87
  276.4 15.2 %convert_reduce_fusion = (f32[3072]{0:T(1024)S(1)}, bf16[1024,3072]{1,0:T(8,128)(2,1)S(1)}) fusion(bf16[1024,768]{0,1:T(8,128)(2,1)S(1)} %get-tuple-element.100, bf16[3072,768]{1,0:T(8,128)(2,1)S(1)} %bitcast.79, f32[1024,3072]{1,0:T(8,128)} %get-tuple-element.119, f32[3072]{0:T(1024)S(1)} %convert_element_type.177), kind=kOutput, calls=%fused_computation.9 | convolution fusion | flops 4882166784 | bytes 25190400 | tf_op jit(solution)/shard_map/dot_general | solution.py:157
  291.6 6.9 multiply_reduce_fusion.1
  310.3 4.0 reshape.170
  314.3 18.2 %multiply_reduce_fusion = (f32[2,12,512]{2,1,0:T(8,128)S(1)}, f32[2,12,512,512]{2,3,1,0:T(8,128)}) fusion(f32[2,12,512]{2,1,0:T(8,128)S(1)} %log_add_fusion, f32[2,12,512,512]{2,3,1,0:T(8,128)} %get-tuple-element.117, pred[2,512,512]{1,2,0:T(8,128)(4,1)S(1)} %copy-done.3, bf16[2,512,12,64]{1,0,3,2:T(2,128)(2,1)S(1)} %copy-done.11, ...), kind=kOutput, calls=%fused_computation.1 | convolution fusion | flops 836751360 | bytes 54099968 | tf_op jit(solution)/shard_map/sqhe,skhe->shqk/dot_general | solution.py:177
  332.6 21.9 %multiply_convert_fusion = bf16[2,12,512,512]{2,3,1,0:T(8,128)(2,1)} fusion(f32[2,12,512,512]{2,3,1,0:T(8,128)} %get-tuple-element.122, f32[2,12,512]{2,1,0:T(8,128)S(1)} %get-tuple-element.121, f32[2,12,512]{2,1,0:T(8,128)S(1)} %log_add_fusion, f32[2,12,512,512]{2,3,1,0:T(8,128)} %get-tuple-element.117, pred[2,512,512]{1,2,0:T(8,128)(4,1)S(1)} %copy-done.3), kind=kLoop, calls=%fused_computation | loop fusion | flops 37748736 | bytes 63537152 | tf_op jit(solution)/shard_map/convert_element_type | solution.py:184
  354.5 12.2 %convert_reduce_fusion.4 = (f32[12,64]{1,0:T(8,128)S(1)}, bf16[2,512,12,64]{1,3,2,0:T(8,128)(2,1)S(1)}) fusion(f32[2,12,512]{2,1,0:T(8,128)S(1)} %log_add_fusion, f32[2,12,512,512]{2,3,1,0:T(8,128)} %get-tuple-element.117, pred[2,512,512]{1,2,0:T(8,128)(4,1)S(1)} %copy-done.3, bf16[2,512,12,64]{1,0,3,2:T(2,128)(2,1)S(1)} %copy-done.12), kind=kOutput, calls=%fused_computation.34 | convolution fusion | flops 832830720 | bytes 28888064 | tf_op jit(solution)/shard_map/shqk,sqhe->skhe/dot_general | solution.py:180
  368.7 8.6 %fusion.21 = bf16[2,512,12,64]{1,3,2,0:T(8,128)(2,1)S(1)} fusion(bf16[2,12,512,512]{2,3,1,0:T(8,128)(2,1)} %multiply_convert_fusion, bf16[2,512,12,64]{1,0,3,2:T(2,128)(2,1)S(1)} %copy-done.2), kind=kOutput, calls=%fused_computation.61 | convolution fusion | flops 806879232 | bytes 15728640 | tf_op jit(solution)/shard_map/shqk,sqhe->skhe/dot_general | solution.py:190
  379.4 7.0 convert_reduce_fusion.5
  391.1 5.8 convolution_bitcast_fusion
  396.9 8.2 copy.112
  407.1 10.5 %fusion.43 = f32[768,3072]{1,0:T(8,128)} fusion(bf16[1024,3072]{1,0:T(8,128)(2,1)} %copy-done.23, f32[1024,768]{0,1:T(8,128)S(1)} %copy-done.8, f32[768]{0:T(1024)S(1)} %convert_element_type.174, f32[768]{0:T(1024)S(1)} %convert_element_type.173, f32[1024]{0:T(1024)S(1)} %fusion.33, f32[1024]{0:T(1024)S(1)} %broadcast_multiply_fusion.1), kind=kOutput, calls=%fused_computation.104 | convolution fusion | flops 4835770368 | bytes 18888704 | tf_op jit(solution)/shard_map/dot_general | solution.py:161
  419.0 10.2 %fusion.46 = f32[3072,768]{1,0:T(8,128)} fusion(bf16[1024,3072]{1,0:T(8,128)(2,1)} %get-tuple-element.118, bf16[1024,768]{0,1:T(8,128)(2,1)S(1)} %copy-done.17), kind=kOutput, calls=%fused_computation.107 | convolution fusion | flops 4831838208 | bytes 17301504 | tf_op jit(solution)/shard_map/dot_general | solution.py:156
  433.3 40.5 %all-reduce.18 = (f32[4]{0:T(128)S(1)}, f32[]{:T(128)}, f32[768]{0:T(1024)S(1)}, f32[768]{0:T(1024)S(1)}, f32[768]{0:T(1024)S(1)}, /*index=5*/f32[768]{0:T(1024)...) all-reduce(f32[4]{0:T(128)S(1)} %pad_maximum_fusion, ...), channel_id=1, replica_groups=mesh['dp'=16,'fsdp'=2] {'dp','fsdp'}, use_global_device_ids=true, to_apply=%region_19.20 | all-reduce | flops 9221 | bytes 73768 | tf_op jit(solution)/shard_map/psum | solution.py:271
  481.0 8.9 %add_add_fusion.2 = f32[1024,768]{0,1:T(8,128)} fusion(f32[1024,768]{0,1:T(8,128)S(1)} %copy-done.5, bf16[768,2304]{1,0:T(8,128)(2,1)} %all-gather.5.cloned.1.call-done, bf16[1024,2304]{0,1:T(8,128)(2,1)} %copy-done.19, f32[1024]{0:T(1024)S(1)} %negate_multiply_fusion), kind=kOutput, calls=%fused_computation.49 | convolution fusion | flops 3625451520 | bytes 14553088 | tf_op jit(solution)/shard_map/dot_general | solution.py:199
  495.2 42.5 %reduce-scatter.13.cloned.1.call-done = f32[24,2304]{1,0:T(8,128)} async-done(((f32[768,2304]{1,0:T(8,128)}), f32[24,2304]{1,0:T(8,128)}) %reduce-scatter.13.cloned.1.call-update) | async-done | bytes 221200
  537.8 141.3 %reduce-scatter.9.cloned.1.call-done = f32[24,3072]{1,0:T(8,128)} async-done(((f32[768,3072]{1,0:T(8,128)}), f32[24,3072]{1,0:T(8,128)}) %reduce-scatter.9.cloned.1.call-update) | async-done | bytes 294928 | tf_op jit(solution)/shard_map/reduce_scatter | solution.py:298
  679.1 142.1 %reduce-scatter.11.cloned.1.call-done = f32[96,768]{1,0:T(8,128)} async-done(((f32[3072,768]{1,0:T(8,128)}), f32[96,768]{1,0:T(8,128)}) %reduce-scatter.11.cloned.1.call-update) | async-done | bytes 294928 | tf_op jit(solution)/shard_map/reduce_scatter | solution.py:300
  (160 shorter events, 76.4 us)
Async XLA Ops:
  7.2 55.5 %copy-start.13 = (bf16[1024,768]{1,0:T(8,128)(2,1)S(1)}, bf16[1024,768]{1,0:T(8,128)(2,1)}, u32[]{:S(2)}) copy-start(bf16[1024,768]{1,0:T(8,128)(2,1)} %param.17) | copy-start | bytes 4718596
  7.2 66.9 %all-gather.5.cloned.1.call-start = ((), (), s32[]{:S(2)}) async-start(), calls=%async_computation.4 | async-start | bytes 3649536 | tf_op jit(solution)/shard_map/all_gather | solution.py:255
  7.9 137.3 %all-gather.7.cloned.1.call-start = ((), (), s32[]{:S(2)}) async-start(), calls=%async_computation.5 | async-start | bytes 1216512 | tf_op jit(solution)/shard_map/all_gather | solution.py:258
  8.7 186.8 %all-gather.9.cloned.1.call-start = ((), (), s32[]{:S(2)}) async-start(), calls=%async_computation.6 | async-start | bytes 4866048 | tf_op jit(solution)/shard_map/all_gather | solution.py:262
  9.4 251.3 %all-gather.11.cloned.1.call-start = ((), (), s32[]{:S(2)}) async-start(), calls=%async_computation.7 | async-start | bytes 4866048 | tf_op jit(solution)/shard_map/all_gather | solution.py:264
  10.0 485.2 %reduce-scatter.7.cloned.1.call-start = ((), (), s32[]{:S(2)}) async-start(), calls=%async_computation.8 | async-start | bytes 2433024 | tf_op jit(solution)/shard_map/reduce_scatter | solution.py:294
  61.0 3.4 copy-start.20
  79.9 3.6 copy-start.9
  88.2 12.1 %copy-start = (bf16[2,512,12,64]{1,0,3,2:T(2,128)(2,1)}, bf16[2,512,12,64]{1,0,3,2:T(2,128)(2,1)S(1)}, u32[]{:S(2)}) copy-start(bf16[2,512,12,64]{1,0,3,2:T(2,128)(2,1)S(1)} %reshape.168) | copy-start | bytes 4718596
  112.3 6.5 copy-start.3
  118.8 11.2 %copy-start.10 = (bf16[2,512,12,64]{1,0,3,2:T(2,128)(2,1)S(1)}, bf16[2,512,12,64]{1,0,3,2:T(2,128)(2,1)}, u32[]{:S(2)}) copy-start(bf16[2,512,12,64]{1,0,3,2:T(2,128)(2,1)} %reshape.166) | copy-start | bytes 4718596
  149.9 1.7 copy-start.6
  270.6 5.8 slice-start.2
  271.7 4.6 slice-start.3
  273.6 18.0 %slice-start = ((s8[4718592]{0:T(1024)(128)(4,1)}), s8[4194304]{0:T(1024)(128)(4,1)S(1)}, s32[]{:S(2)}) async-start(s8[4718592]{0:T(1024)(128)(4,1)} %bitcast.76), calls=%async_computation.12 | async-start | bytes 8388608
  276.3 15.2 %copy-start.16 = (bf16[1024,768]{0,1:T(8,128)(2,1)}, bf16[1024,768]{0,1:T(8,128)(2,1)S(1)}, u32[]{:S(2)}) copy-start(bf16[1024,768]{0,1:T(8,128)(2,1)S(1)} %get-tuple-element.100) | copy-start | bytes 4718596
  276.3 15.2 %copy-start.7 = (f32[1024,768]{0,1:T(8,128)S(1)}, f32[1024,768]{0,1:T(8,128)}, u32[]{:S(2)}) copy-start(f32[1024,768]{0,1:T(8,128)} %copy-done.6) | copy-start | bytes 9437188
  276.4 15.2 %slice-start.1 = ((s8[4718592]{0:T(1024)(128)(4,1)}), s8[524288]{0:T(1024)(128)(4,1)S(1)}, s32[]{:S(2)}) async-start(s8[4718592]{0:T(1024)(128)(4,1)} %bitcast.76), calls=%async_computation.13 | async-start | bytes 1048576
  291.6 6.9 copy-start.23
  299.3 1.8 copy-start.4
  299.3 3.3 copy-start.15
  310.3 4.1 copy-start.11
  314.3 223.5 %reduce-scatter.13.cloned.1.call-start = ((), (), s32[]{:S(2)}) async-start(), calls=%async_computation.11 | async-start | bytes 7299072
  332.6 21.9 %copy-start.12 = (bf16[2,512,12,64]{1,0,3,2:T(2,128)(2,1)S(1)}, bf16[2,512,12,64]{1,0,3,2:T(2,128)(2,1)}, u32[]{:S(2)}) copy-start(bf16[2,512,12,64]{1,0,3,2:T(2,128)(2,1)} %reshape.170) | copy-start | bytes 4718596
  366.7 2.1 copy-start.2
  377.4 2.1 copy-start.1
  388.6 2.5 copy-start.14
  388.8 2.3 copy-start.19
  405.2 1.9 copy-start.8
  405.2 273.9 %reduce-scatter.9.cloned.1.call-start = ((), (), s32[]{:S(2)}) async-start(), calls=%async_computation.9 | async-start | bytes 9732096 | tf_op jit(solution)/shard_map/reduce_scatter | solution.py:298
  417.6 403.6 %reduce-scatter.11.cloned.1.call-start = ((), (), s32[]{:S(2)}) async-start(), calls=%async_computation.10 | async-start | bytes 9732096 | tf_op jit(solution)/shard_map/reduce_scatter | solution.py:300
  429.2 51.8 %copy-start.5 = (f32[1024,768]{0,1:T(8,128)S(1)}, f32[1024,768]{0,1:T(8,128)}, u32[]{:S(2)}) copy-start(f32[1024,768]{0,1:T(8,128)} %copy-done.4) | copy-start | bytes 9437188
  (4 other events, 4.1 us)
Sparse Core Ops, SparseCore 0:
  10.9 63.0 all-gather.4
  77.0 52.8 all-gather.6
  132.8 62.5 all-gather.8
  198.2 62.4 all-gather.10
  314.4 97.8 reduce-scatter.6
  419.3 118.4 reduce-scatter.12
  544.2 134.8 reduce-scatter.8
  686.6 134.6 reduce-scatter.10
where the time goes:
time: 838 us; the launch traced here: 829 us
  waiting for transfers between devices  432 us (52%)
  matrix products  167 us (20%)
  blocking collectives  83 us (10%)
  local copies, waits for them, and re-layouts  77.8 us (9%)
  other arithmetic  52 us (6%)
  between operations  15.8 us (2%)
    reduce_scatter x1, waiting for transfers between devices, per_device(): lax.psum_scatter(gradients[9], ('dp', 'fsdp'), scatter_dimension=0, tiled...  142 us
    reduce_scatter x1, waiting for transfers between devices, per_device(): lax.psum_scatter(gradients[7], ('dp', 'fsdp'), scatter_dimension=0, tiled...  141 us
    all_gather x1, waiting for transfers between devices, per_device(): lax.all_gather(shards[9], ('dp', 'fsdp'), axis=0, tiled=True)  51.7 us
    unnamed x94, local copies, waits for them, and re-layouts  47.8 us
    unnamed x9, waiting for transfers between devices  45.2 us
    all_gather x1, waiting for transfers between devices, per_device(): lax.all_gather(shards[7], ('dp', 'fsdp'), axis=0, tiled=True)  43.5 us
    unnamed x1, blocking collectives  42.5 us
    psum x1, blocking collectives, per_device(): total_sums, total_count = lax.psum((stat_sums, local_count), ('dp', 'fsdp'))  40.5 us
  transfers between devices with their start and end apart: 8, of which 6 were waited for; matrix products, arithmetic and copies ran while one was open for 28% of the time, Pallas kernels for 0%

commit v1 on v0

--- a/solution.py
+++ b/solution.py
@@ -1,9 +1,263 @@
+import functools
+
 import jax
 import jax.numpy as jnp
 from jax import lax
+from jax.experimental import pallas as pl
+from jax.experimental.pallas import tpu as pltpu
 from jax.sharding import PartitionSpec as P
 
 HEAD_DIM = 64
+BLOCKS = 32
+
+MESH = pl.DeviceIdType.MESH
+ALL = slice(None)
+
+class Net:
+    def __init__(self, Z, Y):
+        self.Z, self.Y = Z, Y
+        dp, y = lax.axis_index("dp"), lax.axis_index("fsdp")
+        self.fs = y
+        self.at = {"z": dp // 4, "x": (dp // 2) % 2, "c": dp % 2, "y": y if Y == 2 else 0}
+    def device(self, **moved):
+        p = dict(self.at, **moved)
+        return (p["z"] * 4 + p["x"] * 2 + p["c"], p["y"] if self.Y == 2 else self.fs)
+    def across(self, axis):
+        return self.device(**{axis: 1 - self.at[axis]})
+    def barrier(self):
+        bar = pltpu.get_barrier_semaphore()
+        z, Z = self.at["z"], self.Z
+        others = [self.across(axis) for axis in (["c", "x"] + (["y"] if self.Y == 2 else []))]
+        others += [self.device(z=(z + k) % Z) for k in range(1, Z)]
+        for other in others:
+            pl.semaphore_signal(bar, inc=1, device_id=other, device_id_type=MESH)
+        pl.semaphore_wait(bar, len(others))
+
+def orders(Y):
+    o = ["zxy", "xyz", "yzx"]
+    return o if Y == 2 else [k.replace("y", "") for k in o]
+
+def n_sems(Z):
+    return 3 * 3 * 2 * max(1, Z - 1) + 1
+
+def sem_id(Z, part, phase, step=0, down=0):
+    return ((part * 3 + phase) * 2 + down) * max(1, Z - 1) + step
+
+def gather_stages(net, buf, cols, ss, rs):
+    Z, Y = net.Z, net.Y
+    at = net.at
+    def ref(idx, col):
+        return buf.at[at["c"], idx["x"], idx["y"], idx["z"], :, pl.ds(*col)]
+    def copy(idx, col, sem, device):
+        r = ref(idx, col)
+        return pltpu.make_async_remote_copy(src_ref=r, dst_ref=r, send_sem=ss.at[sem], recv_sem=rs.at[sem], device_id=device, device_id_type=MESH)
+    ords = orders(Y)
+    chains = []
+    for part, order in enumerate(ords):
+        col = cols[part]
+        if col[1] == 0:
+            continue
+        steps = []
+        done = set()
+        for phase, axis in enumerate(order):
+            base = {k: (ALL if k in done else at[k]) for k in "xyz"}
+            if axis != "z":
+                def make(base=base, col=col, axis=axis, sem=sem_id(Z, part, phase)):
+                    mk = lambda: copy(base, col, sem, net.across(axis))
+                    return (lambda: mk().start(), lambda: mk().wait_recv(), lambda: mk().wait_send())
+                steps.append((phase, make()))
+            else:
+                for s in range(Z - 1):
+                    def make(base=base, col=col, s=s, su=sem_id(Z, part, phase, s, 0), sd=sem_id(Z, part, phase, s, 1)):
+                        z = at["z"]
+                        up = lambda: copy(dict(base, z=z - s), col, su, net.device(z=z + 1))
+                        dn = lambda: copy(dict(base, z=z + s), col, sd, net.device(z=z - 1))
+                        can_up = (z - s >= 0) & (z + 1 < Z)
+                        can_dn = (z + s < Z) & (z > 0)
+                        ru = lambda: copy(dict(base, z=z - 1 - s), col, su, net.device(z=z - 1))
+                        rd = lambda: copy(dict(base, z=z + 1 + s), col, sd, net.device(z=z + 1))
+                        got_u, got_d = z - 1 - s >= 0, z + 1 + s < Z
+                        def start():
+                            pl.when(can_up)(lambda: up().start())
+                            pl.when(can_dn)(lambda: dn().start())
+                        def recv():
+                            pl.when(got_u)(lambda: ru().wait_recv())
+                            pl.when(got_d)(lambda: rd().wait_recv())
+                        def send():
+                            pl.when(can_up)(lambda: up().wait_send())
+                            pl.when(can_dn)(lambda: dn().wait_send())
+                        return start, recv, send
+                    steps.append((phase, make()))
+            done.add(axis)
+        chains.append(steps)
+    whole = cols[3]
+    core_sem = n_sems(Z) - 1
+    def core_copy():
+        r = buf.at[at["c"], :, :, :, :, pl.ds(*whole)]
+        return pltpu.make_async_remote_copy(src_ref=r, dst_ref=r, send_sem=ss.at[core_sem], recv_sem=rs.at[core_sem], device_id=net.across("c"), device_id_type=MESH)
+    def core_recv():
+        r = buf.at[1 - at["c"], :, :, :, :, pl.ds(*whole)]
+        return pltpu.make_async_remote_copy(src_ref=r, dst_ref=r, send_sem=ss.at[core_sem], recv_sem=rs.at[core_sem], device_id=net.across("c"), device_id_type=MESH)
+    return chains, core_copy, core_recv
+
+def run_sync(chains):
+    stages = []
+    for phase in range(3):
+        subs = [[st for ph, st in ch if ph == phase] for ch in chains]
+        n = max(len(s) for s in subs)
+        for k in range(n):
+            def stage(k=k, subs=subs):
+                for s in subs:
+                    if k < len(s):
+                        if k > 0:
+                            s[k - 1][1]()
+                        s[k][0]()
+            stages.append(stage)
+        def last(subs=subs):
+            for s in subs:
+                if s:
+                    s[-1][1]()
+        stages.append(last)
+    return stages
+
+def run_async(chains):
+    stages = []
+    n = max(len(c) for c in chains)
+    for k in range(n + 1):
+        def stage(k=k):
+            for ch in chains:
+                if 0 < k <= len(ch):
+                    ch[k - 1][1][1]()
+                if k < len(ch):
+                    ch[k][1][0]()
+        stages.append(stage)
+    return stages
+
+
+def add_into(dst, src, lead):
+    total = 1
+    for n in lead:
+        total *= n
+    def one(i, carry):
+        idx = []
+        for n in reversed(lead):
+            idx.append(i % n); i = i // n
+        idx = tuple(reversed(idx))
+        dst[idx] = (dst[idx].astype(jnp.float32) + src[idx].astype(jnp.float32)).astype(dst.dtype)
+        return carry
+    if total == 1:
+        one(0, 0)
+    else:
+        lax.fori_loop(0, total, one, 0)
+
+def scatter_scratch(Z, Y, cols, R=48):
+    size = {"x": 2, "y": Y, "z": Z}
+    out = []
+    for part, order in enumerate(orders(Y)):
+        w = cols[part][1]
+        out.append(pltpu.VMEM((2, Y, Z, R, w), jnp.bfloat16))
+        free = [k for k in order]
+        for axis in reversed(order):
+            free.remove(axis)
+            lead = tuple(size[k] for k in "xyz" if k in free)
+            if axis == "z":
+                out.append(pltpu.VMEM((2, Z - 1) + lead + (R, w), jnp.bfloat16))
+            else:
+                out.append(pltpu.VMEM(lead + (R, w), jnp.bfloat16))
+    return out
+
+def scatter_chains(net, buf, cols, scratch, ss, rs):
+    Z, Y = net.Z, net.Y
+    at = net.at
+    size = {"x": 2, "y": Y, "z": Z}
+    chains = []
+    scratch = list(scratch)
+    for part, order in enumerate(orders(Y)):
+        col = pl.ds(*cols[part])
+        bufs = [scratch.pop(0) for _ in range(len(order) + 1)]
+        steps = []
+        def ref(c, idx, col=col):
+            return buf.at[c, idx["x"], idx["y"] if Y == 2 else 0, idx["z"], :, col]
+        def rc(src, dst, sem, device):
+            return pltpu.make_async_remote_copy(src_ref=src, dst_ref=dst, send_sem=ss.at[sem], recv_sem=rs.at[sem], device_id=device, device_id_type=MESH)
+        def lead_of(free):
+            return tuple(size[k] for k in "xyz" if k in free)
+        allidx = {k: ALL for k in "xyz"}
+        if Y != 2:
+            allidx["y"] = 0
+        def make_core(rb=bufs[0], part=part, ref=ref):
+            sem = n_sems(Z) - 1 + part
+            rbv = rb if Y == 2 else rb.at[:, 0]
+            mk = lambda: rc(ref(1 - at["c"], allidx), rbv, sem, net.across("c"))
+            def recv():
+                mk().wait_recv()
+                add_into(ref(at["c"], allidx), rbv, lead_of([k for k in "xyz" if k in order]))
+            return (lambda: mk().start(), recv, lambda: mk().wait_send())
+        steps.append((0, make_core()))
+        free = list(order)
+        for phase, axis in enumerate(reversed(order)):
+            free.remove(axis)
+            base = {k: (ALL if k in free else at[k]) for k in "xyz"}
+            rb = bufs[1 + phase]
+            lead = lead_of(free)
+            if axis != "z":
+                def make(base=base, axis=axis, rb=rb, lead=lead, sem=sem_id(Z, part, phase), ref=ref):
+                    mk = lambda: rc(ref(at["c"], dict(base, **{axis: 1 - at[axis]})), rb, sem, net.across(axis))
+                    def recv():
+                        mk().wait_recv()
+                        add_into(ref(at["c"], dict(base, **{axis: at[axis]})), rb, lead)
+                    return (lambda: mk().start(), recv, lambda: mk().wait_send())
+                steps.append((phase + 1, make()))
+            else:
+                for s in range(Z - 1):
+                    def make(base=base, rb=rb, lead=lead, s=s, su=sem_id(Z, part, phase, s, 0), sd=sem_id(Z, part, phase, s, 1), ref=ref):
+                        z = at["z"]
+                        zr = Z - 1 - z
+                        can_up = (z <= s) & (z < Z - 1)
+                        can_dn = (zr <= s) & (z > 0)
+                        up = lambda: rc(ref(at["c"], dict(base, z=Z - 1 - s + z)), rb.at[0, s], su, net.device(z=z + 1))
+                        dn = lambda: rc(ref(at["c"], dict(base, z=s - zr)), rb.at[1, s], sd, net.device(z=z - 1))
+                        got_u = (z - 1 <= s) & (z > 0)
+                        got_d = (zr - 1 <= s) & (zr > 0)
+                        def start():
+                            pl.when(can_up)(lambda: up().start())
+                            pl.when(can_dn)(lambda: dn().start())
+                        def recv():
+                            @pl.when(got_u)
+                            def _():
+                                rc(ref(at["c"], dict(base, z=z)), rb.at[0, s], su, net.device(z=z - 1)).wait_recv()
+                                add_into(ref(at["c"], dict(base, z=Z - 2 - s + z)), rb.at[0, s], lead)
+                            @pl.when(got_d)
+                            def _():
+                                rc(ref(at["c"], dict(base, z=z)), rb.at[1, s], sd, net.device(z=z + 1)).wait_recv()
+                                add_into(ref(at["c"], dict(base, z=s + 1 - zr)), rb.at[1, s], lead)
+                        def send():
+                            pl.when(can_up)(lambda: up().wait_send())
+                            pl.when(can_dn)(lambda: dn().wait_send())
+                        return start, recv, send
+                    steps.append((phase + 1, make()))
+        chains.append(steps)
+    return chains
+
+def run_sync4(chains):
+    stages = []
+    for phase in range(4):
+        subs = [[st for ph, st in ch if ph == phase] for ch in chains]
+        n = max(len(s) for s in subs)
+        for k in range(n):
+            def stage(k=k, subs=subs):
+                for s in subs:
+                    if k < len(s):
+                        if k > 0:
+                            s[k - 1][1]()
+                        s[k][0]()
+            stages.append(stage)
+        def last(subs=subs):
+            for s in subs:
+                if s:
+                    s[-1][1]()
+        stages.append(last)
+    return stages
 
 
 def layer_norm(value, gain, shift):
@@ -217,7 +471,144 @@
     return (token_grad, gradients)
 
 
+def tiles_of(counts, first=0):
+    out, at = [], first
+    for count in counts:
+        out.append((at * 128, count * 128))
+        at += count
+    return out + [(first * 128, sum(counts) * 128)]
+
+
+GATHERED = tiles_of((14, 9, 14))
+SCATTERED = tiles_of((14, 9, 13))
+
+
+def gather_kernel(Z, Y, own_ref, all_ref, ss, rs, ls):
+    net = Net(Z, Y)
+    at = net.at
+    own = all_ref.at[at["c"], at["x"], at["y"], at["z"]]
+    load = pltpu.make_async_copy(own_ref, own, ls)
+    load.start()
+    net.barrier()
+    load.wait()
+    chains, core_copy, core_recv = gather_stages(net, all_ref, GATHERED, ss, rs)
+    for stage in run_sync(chains):
+        stage()
+    core_copy().start()
+    core_recv().wait_recv()
+    for chain in chains:
+        for _, step in chain:
+            step[2]()
+    core_copy().wait_send()
+
+
+def gather_all(block, Z, Y):
+    count = n_sems(Z)
+    return pl.pallas_call(
+        functools.partial(gather_kernel, Z, Y),
+        out_shape=jax.ShapeDtypeStruct((2, 2, Y, Z) + block.shape, block.dtype),
+        in_specs=[pl.BlockSpec(memory_space=pl.ANY)],
+        out_specs=pl.BlockSpec(memory_space=pl.ANY),
+        scratch_shapes=[
+            pltpu.SemaphoreType.DMA((count,)),
+            pltpu.SemaphoreType.DMA((count,)),
+            pltpu.SemaphoreType.DMA,
+        ],
+        compiler_params=pltpu.CompilerParams(
+            collective_id=0, has_side_effects=True, vmem_limit_bytes=60 * 2**20
+        ),
+        name="gather",
+    )(block)
+
+
+def small_steps(net, Z, Y):
+    at = net.at
+    out = [lambda: net.across("c"), lambda: net.across("x")]
+    if Y == 2:
+        out.append(lambda: net.across("y"))
+    bit = 1
+    while bit < Z:
+        def partner(bit=bit):
+            low = (at["z"] // bit) % 2
+            return net.device(z=at["z"] + bit - 2 * bit * low)
+        out.append(partner)
+        bit *= 2
+    return out
+
+
+def scatter_kernel(Z, Y, parts_ref, small_ref, own_ref, sum_ref, buf, mine, theirs, ss, rs, sss, srs, ls, *scratch):
+    net = Net(Z, Y)
+    at = net.at
+    load = pltpu.make_async_copy(parts_ref, buf, ls)
+    load.start()
+    mine[0] = small_ref[...]
+    net.barrier()
+    load.wait()
+    chains = scatter_chains(net, buf, SCATTERED, scratch, ss, rs)
+    stages = run_sync4(chains)
+    partners = small_steps(net, Z, Y)
+    copies = [
+        pltpu.make_async_remote_copy(
+            src_ref=mine.at[k], dst_ref=theirs.at[k], send_sem=sss.at[k], recv_sem=srs.at[k],
+            device_id=partner(), device_id_type=MESH,
+        )
+        for k, partner in enumerate(partners)
+    ]
+    for k, stage in enumerate(stages):
+        stage()
+        if 0 < k <= len(copies):
+            copies[k - 1].wait_recv()
+            mine[k] = mine[k - 1] + theirs[k - 1]
+        if k < len(copies):
+            copies[k].start()
+    sum_ref[...] = mine[len(copies)]
+    for copy in copies:
+        copy.wait_send()
+    for chain in chains:
+        for _, step in chain:
+            step[2]()
+    own_ref[...] = buf[at["c"], at["x"], at["y"], at["z"]].astype(jnp.float32)
+
+
+def scatter_all(parts, small, Z, Y):
+    count = n_sems(Z) + 3
+    rounds = 2 + (Y == 2) + (Z - 1).bit_length()
+    assert 2 ** (Z - 1).bit_length() == Z
+    return pl.pallas_call(
+        functools.partial(scatter_kernel, Z, Y),
+        out_shape=(
+            jax.ShapeDtypeStruct(parts.shape[4:], jnp.float32),
+            jax.ShapeDtypeStruct(small.shape, jnp.float32),
+        ),
+        in_specs=[pl.BlockSpec(memory_space=pl.ANY), pl.BlockSpec(memory_space=pltpu.VMEM)],
+        out_specs=[pl.BlockSpec(memory_space=pltpu.VMEM)] * 2,
+        scratch_shapes=[
+            pltpu.VMEM(parts.shape, jnp.bfloat16),
+            pltpu.VMEM((rounds + 1,) + small.shape, jnp.float32),
+            pltpu.VMEM((rounds,) + small.shape, jnp.float32),
+            pltpu.SemaphoreType.DMA((count,)),
+            pltpu.SemaphoreType.DMA((count,)),
+            pltpu.SemaphoreType.DMA((rounds,)),
+            pltpu.SemaphoreType.DMA((rounds,)),
+            pltpu.SemaphoreType.DMA,
+        ]
+        + scatter_scratch(Z, Y, SCATTERED),
+        compiler_params=pltpu.CompilerParams(
+            collective_id=1, has_side_effects=True, vmem_limit_bytes=60 * 2**20
+        ),
+        name="scatter",
+    )(parts, small)
+
+
+def fold(rows):
+    half = rows.shape[1] // 2
+    return jnp.concatenate([rows[:, :half], rows[:, half:]], axis=0)
+
+
 def per_device(
+    Z,
+    Y,
+    fsdp,
     tokens,
     segment_ids,
     valid,
@@ -236,93 +627,113 @@
     second_shift,
     cotangent,
 ):
-    shards = (
-        input_weight,
-        query_bias,
-        value_bias,
-        output_weight,
-        output_bias,
-        first_gain,
-        first_shift,
-        expand_weight,
-        expand_bias,
-        shrink_weight,
-        shrink_bias,
-        second_gain,
-        second_shift,
-    )
+    vectors = (query_bias, value_bias, output_bias, first_gain, first_shift, shrink_bias, second_gain, second_shift)
+    matrices = (input_weight, output_weight, expand_weight, shrink_weight)
+    if Y == 1 and fsdp > 1:
+        def whole(v):
+            return lax.all_gather(v, "fsdp", axis=0, tiled=True)
+        vectors, matrices, expand_bias = tuple(map(whole, vectors)), tuple(map(whole, matrices)), whole(expand_bias)
+    rows = vectors[0].shape[0]
+    features = tokens.shape[1]
+    small = jnp.concatenate([jnp.stack(vectors), expand_bias.reshape(4, rows)], axis=0)
+    small = jnp.pad(small, ((0, 2 * rows - 12), (0, 128 - rows)))
+    last = matrices[3]
+    last = jnp.concatenate([last[: 2 * rows], last[2 * rows :]], axis=1)
+    block = jnp.concatenate([fold(matrices[0]), small, fold(matrices[1]), fold(matrices[2]), last], axis=1)
+    gathered = gather_all(block, Z, Y)
+    gathered = gathered.transpose(3, 1, 0, 2, 4, 5).reshape((BLOCKS,) + block.shape)
+
+    def unfold(part):
+        half = part.shape[2]
+        return part.reshape(BLOCKS, 2, rows, half).transpose(0, 2, 1, 3).reshape(BLOCKS * rows, 2 * half)
+
+    small = gathered[:, :12, 1152 : 1152 + rows]
+    vector = small[:, :8].transpose(1, 0, 2).reshape(8, features)
+    full_expand_bias = small[:, 8:].reshape(-1)
+    full_last = gathered[:, :, 3200:].reshape(BLOCKS, 2 * rows, 2, features).transpose(0, 2, 1, 3).reshape(-1, features)
     params = (
-        lax.all_gather(shards[0], ("dp", "fsdp"), axis=0, tiled=True),
-        lax.all_gather(shards[1], ("dp", "fsdp"), axis=0, tiled=True),
-        lax.all_gather(shards[2], ("dp", "fsdp"), axis=0, tiled=True),
-        lax.all_gather(shards[3], ("dp", "fsdp"), axis=0, tiled=True),
-        lax.all_gather(shards[4], ("dp", "fsdp"), axis=0, tiled=True),
-        lax.all_gather(shards[5], ("dp", "fsdp"), axis=0, tiled=True),
-        lax.all_gather(shards[6], ("dp", "fsdp"), axis=0, tiled=True),
-        lax.all_gather(shards[7], ("dp", "fsdp"), axis=0, tiled=True),
-        lax.all_gather(shards[8], ("dp", "fsdp"), axis=0, tiled=True),
-        lax.all_gather(shards[9], ("dp", "fsdp"), axis=0, tiled=True),
-        lax.all_gather(shards[10], ("dp", "fsdp"), axis=0, tiled=True),
-        lax.all_gather(shards[11], ("dp", "fsdp"), axis=0, tiled=True),
-        lax.all_gather(shards[12], ("dp", "fsdp"), axis=0, tiled=True),
+        unfold(gathered[:, :, :1152]),
+        vector[0],
+        vector[1],
+        unfold(gathered[:, :, 1280:1664]),
+        vector[2],
+        vector[3],
+        vector[4],
+        unfold(gathered[:, :, 1664:3200]),
+        full_expand_bias,
+        full_last,
+        vector[5],
+        vector[6],
+        vector[7],
     )
     result, stat_sums, stored = forward_pass(params, tokens, segment_ids, valid)
     local_count = jnp.sum(valid, dtype=jnp.float32)
-    total_sums, total_count = lax.psum((stat_sums, local_count), ("dp", "fsdp"))
-    statistics = total_sums / (tokens.shape[1] * total_count)
-    params = (
-        lax.all_gather(shards[0], ("dp", "fsdp"), axis=0, tiled=True),
-        lax.all_gather(shards[1], ("dp", "fsdp"), axis=0, tiled=True),
-        lax.all_gather(shards[2], ("dp", "fsdp"), axis=0, tiled=True),
-        lax.all_gather(shards[3], ("dp", "fsdp"), axis=0, tiled=True),
-        lax.all_gather(shards[4], ("dp", "fsdp"), axis=0, tiled=True),
-        lax.all_gather(shards[5], ("dp", "fsdp"), axis=0, tiled=True),
-        lax.all_gather(shards[6], ("dp", "fsdp"), axis=0, tiled=True),
-        lax.all_gather(shards[7], ("dp", "fsdp"), axis=0, tiled=True),
-        lax.all_gather(shards[8], ("dp", "fsdp"), axis=0, tiled=True),
-        lax.all_gather(shards[9], ("dp", "fsdp"), axis=0, tiled=True),
-        lax.all_gather(shards[10], ("dp", "fsdp"), axis=0, tiled=True),
-        lax.all_gather(shards[11], ("dp", "fsdp"), axis=0, tiled=True),
-        lax.all_gather(shards[12], ("dp", "fsdp"), axis=0, tiled=True),
-    )
-    unused_result, unused_sums, stored = forward_pass(params, tokens, segment_ids, valid)
     token_grad, gradients = backward_pass(params, tokens, stored, cotangent)
-    owned = (
-        lax.psum_scatter(gradients[0], ("dp", "fsdp"), scatter_dimension=0, tiled=True),
-        lax.psum_scatter(gradients[1], ("dp", "fsdp"), scatter_dimension=0, tiled=True),
-        lax.psum_scatter(gradients[2], ("dp", "fsdp"), scatter_dimension=0, tiled=True),
-        lax.psum_scatter(gradients[3], ("dp", "fsdp"), scatter_dimension=0, tiled=True),
-        lax.psum_scatter(gradients[4], ("dp", "fsdp"), scatter_dimension=0, tiled=True),
-        lax.psum_scatter(gradients[5], ("dp", "fsdp"), scatter_dimension=0, tiled=True),
-        lax.psum_scatter(gradients[6], ("dp", "fsdp"), scatter_dimension=0, tiled=True),
-        lax.psum_scatter(gradients[7], ("dp", "fsdp"), scatter_dimension=0, tiled=True),
-        lax.psum_scatter(gradients[8], ("dp", "fsdp"), scatter_dimension=0, tiled=True),
-        lax.psum_scatter(gradients[9], ("dp", "fsdp"), scatter_dimension=0, tiled=True),
-        lax.psum_scatter(gradients[10], ("dp", "fsdp"), scatter_dimension=0, tiled=True),
-        lax.psum_scatter(gradients[11], ("dp", "fsdp"), scatter_dimension=0, tiled=True),
-        lax.psum_scatter(gradients[12], ("dp", "fsdp"), scatter_dimension=0, tiled=True),
-    )
+    stats = jnp.pad(jnp.concatenate([stat_sums, local_count[None]]), (0, features - 5))
+    small_grads = jnp.stack([gradients[k] for k in (1, 2, 4, 5, 6, 10, 11, 12)])
+    small_grads = jnp.concatenate(
+        [small_grads, gradients[8].reshape(4, features), stats[None], jnp.zeros((3, features), jnp.float32)]
+    )
+
+    def folded(grad):
+        half = grad.shape[1] // 2
+        return grad.reshape(BLOCKS, rows, 2, half).transpose(0, 2, 1, 3).reshape(BLOCKS, 2 * rows, half)
+
+    last = gradients[9].reshape(BLOCKS, 2, 2 * rows, features).transpose(0, 2, 1, 3)
+    parts = jnp.concatenate(
+        [folded(gradients[0]), folded(gradients[3]), folded(gradients[7]), last.reshape(BLOCKS, 2 * rows, -1)],
+        axis=2,
+    ).astype(jnp.bfloat16)
+    parts = parts.reshape((Z, 2, 2, Y) + parts.shape[1:]).transpose(2, 1, 3, 0, 4, 5)
+    own, sums = scatter_all(parts, small_grads, Z, Y)
+
+    def unfolded(part):
+        return jnp.concatenate([part[:rows], part[rows:]], axis=1)
+
+    weights = [
+        unfolded(own[:, :1152]),
+        unfolded(own[:, 1152:1536]),
+        unfolded(own[:, 1536:3072]),
+        jnp.concatenate([own[:, 3072 : 3072 + features], own[:, 3072 + features :]], axis=0),
+    ]
+    device = lax.axis_index("dp") * Y
+    if Y == 2:
+        device = device + lax.axis_index("fsdp")
+    mine = lax.dynamic_slice(sums, (0, device * rows), (8, rows))
+    mine_expand = lax.dynamic_slice(sums[8:12].reshape(-1), (device * 4 * rows,), (4 * rows,))
+    totals = sums[12, :5]
+    vectors = [mine[k] for k in range(8)]
+    if Y == 1 and fsdp > 1:
+        def share(v):
+            return lax.psum_scatter(v, "fsdp", scatter_dimension=0, tiled=True)
+        weights = [share(v) for v in weights]
+        vectors = [share(v) for v in vectors]
+        mine_expand = share(mine_expand)
+        totals = lax.psum(totals, "fsdp")
+    statistics = totals[:4] / (features * totals[4])
     return (
         result.astype(jnp.bfloat16),
         token_grad,
         statistics,
-        owned[0],
-        owned[1],
-        owned[2],
-        owned[3],
-        owned[4],
-        owned[5],
-        owned[6],
-        owned[7],
-        owned[8],
-        owned[9],
-        owned[10],
-        owned[11],
-        owned[12],
+        weights[0],
+        vectors[0],
+        vectors[1],
+        weights[1],
+        vectors[2],
+        vectors[3],
+        vectors[4],
+        weights[2],
+        mine_expand,
+        weights[3],
+        vectors[5],
+        vectors[6],
+        vectors[7],
     )
 
 
 def solution(mesh):
+    dp, fsdp = mesh.shape["dp"], mesh.shape["fsdp"]
+    Z, Y = dp // 4, (2 if dp * fsdp == BLOCKS else 1)
     in_specs = (
         P(("dp", "fsdp"), None),
         P(("dp", "fsdp"), None),
@@ -361,5 +772,5 @@
         P(("dp", "fsdp")),
     )
     return jax.shard_map(
-        per_device, mesh=mesh, in_specs=in_specs, out_specs=out_specs, check_vma=False
-    )
+        functools.partial(per_device, Z, Y, fsdp), mesh=mesh, in_specs=in_specs, out_specs=out_specs, check_vma=False
+    )

time: 838 us -> 582 us (0.69)
  waiting for transfers between devices: 432 us -> 0 us
  Pallas kernels: 0 us -> 200 us
  blocking collectives: 83 us -> 0 us
  local copies, waits for them, and re-layouts: 77.8 us -> 157 us
  matrix products: 167 us -> 149 us
  other arithmetic: 52 us -> 68.2 us
  between operations: 15.8 us -> 2.41 us
    reduce_scatter x3 -> x0, waiting for transfers between devices: 283 us -> none  [the longest x1 142 us: per_device(): lax.psum_scatter(gradients[9], ('dp', 'fsdp'), scatter_dimension=0, tiled...]
    pallas_call x0 -> x2, Pallas kernels: none -> 200 us  [the longest x1 103 us: scatter_all(): pl.pallas_call(functools.partial(scatter_kernel, Z, Y), out_shape=(jax.Sh...]
    all_gather x4 -> x0, waiting for transfers between devices: 104 us -> none  [the longest x1 51.7 us: per_device(): lax.all_gather(shards[9], ('dp', 'fsdp'), axis=0, tiled=True)]
    reshape x0 -> x15, local copies, waits for them, and re-layouts: none -> 45.6 us  [the longest x3 20.3 us: folded(): grad.reshape(BLOCKS, rows, 2, half).transpose(0, 2, 1, 3)]
    unnamed x9 -> x0, waiting for transfers between devices: 45.2 us -> none
    unnamed x1 -> x0, blocking collectives: 42.5 us -> none
    psum x1 -> x0, blocking collectives: 40.5 us -> none  [per_device(): total_sums, total_count = lax.psum((stat_sums, local_count), ('dp', 'fsdp'))]
    concatenate x0 -> x5, local copies, waits for them, and re-layouts: none -> 18.6 us  [the longest x1 11.6 us: per_device(): jnp.concatenate([folded(gradients[0]), folded(gradients[3]), folded(gradi...]
  transfers between devices with their start and end apart: 8 -> 0, of which waited for: 6 -> 0; matrix products, arithmetic and copies ran while one was open for 28% -> 0% of each run, Pallas kernels for 0% -> 0%
where the time goes in v1:
time: 582 us; the launch traced here: 577 us
  Pallas kernels  200 us (34%)
  local copies, waits for them, and re-layouts  157 us (27%)
  matrix products  149 us (26%)
  other arithmetic  68.2 us (12%)
    pallas_call x1, Pallas kernels, scatter_all(): pl.pallas_call(functools.partial(scatter_kernel, Z, Y), out_shape=(jax.Sh...  103 us
    pallas_call x1, Pallas kernels, gather_all(): pl.pallas_call(functools.partial(gather_kernel, Z, Y), out_shape=jax.Shap...  97 us
    unnamed x101, local copies, waits for them, and re-layouts  33.9 us
    convert_element_type x1, other arithmetic, backward_pass(): score_grad = (probabilities * (prob_grad - inner)).astype(jnp.bfloat16)  21.6 us
    reshape x3, local copies, waits for them, and re-layouts, folded(): grad.reshape(BLOCKS, rows, 2, half).transpose(0, 2, 1, 3)  20.3 us
    dot_general x1, matrix products, backward_pass(): jnp.einsum('sqhe,skhe->shqk', attended_grad, value_rows, preferred_elemen...  18 us
    dot_general x1, matrix products, backward_pass(): jnp.einsum('shqk,sqhe->skhe', weights_low, attended_grad, preferred_eleme...  13.3 us
    reshape x3, local copies, waits for them, and re-layouts, unfold(): part.reshape(BLOCKS, 2, rows, half).transpose(0, 2, 1, 3)  12.8 us

profile of v1, /device:TPU:0, one launch (start us, length us, event | category | flops | bytes accessed | tf_op | source)
XLA Modules:
  0.0 577.0 jit_solution(2994588302158111254)
XLA Ops:
  16.7 97.0 %gather.1 = bf16[2,2,2,4,48,4736]{5,4,3,2,1,0:T(8,128)(2,1)} custom-call(bf16[48,4736]{1,0:T(8,128)(2,1)} %slice_dynamic-update-slice_fusion.own_ref), custom_call_target="tpu_custom_call" | custom-call | tf_op jit(solution)/shard_map/gather/pallas_call | solution.py:507
  113.7 6.1 %copy.51 = bf16[4,2,2,2,48,4736]{5,4,3,2,1,0:T(8,128)(2,1)S(1)} copy(bf16[4,2,2,2,48,4736]{5,4,0,3,1,2:T(8,128)(2,1)} %bitcast.149) | data formatting | bytes 29097984 | tf_op jit(solution)/shard_map/transpose | solution.py:644
  119.8 5.2 copy-done
  135.9 6.5 %fusion.52 = (bf16[32,48,1536]{2,1,0:T(8,128)(2,1)S(1)}, bf16[32,48,1536]{2,1,0:T(8,128)(2,1)}) fusion(bf16[32,48,4736]{2,1,0:T(8,128)(2,1)} %bitcast.154), kind=kLoop, calls=%fused_computation.149 | loop fusion | bytes 18874368 | tf_op jit(solution)/shard_map/slice | solution.py:653
  144.8 9.2 %copy.59 = bf16[32,2,24,1536]{3,1,2,0:T(2,128)(2,1)} copy(bf16[32,2,24,1536]{3,2,1,0:T(8,128)(2,1)} %bitcast.158) | data formatting | bytes 9437184 | tf_op jit(solution)/shard_map/reshape | solution.py:648
  153.9 5.7 copy.96
  163.8 4.1 convolution_bitcast_fusion
  171.9 4.2 reshape.323
  179.0 11.6 %fusion.6 = (f32[2,12,512]{2,1,0:T(8,128)S(1)}, f32[2,12,512,512]{2,3,1,0:T(8,128)}) fusion(pred[2,512,512]{1,2,0:T(8,128)(4,1)} %or_and_fusion, bf16[2,512,12,64]{1,0,3,2:T(2,128)(2,1)S(1)} %reshape.325, bf16[2,512,12,64]{1,0,3,2:T(2,128)(2,1)S(1)} %reshape.324), kind=kOutput, calls=%fused_computation.17 | convolution fusion | flops 824168448 | bytes 28884992 | tf_op jit(solution)/shard_map/sqhe,skhe->shqk/dot_general | solution.py:281
  190.7 11.1 %fusion = f32[2,12,512]{2,1,0:T(8,128)S(1)} fusion(f32[2,12,512]{2,1,0:T(8,128)S(1)} %get-tuple-element.116, f32[2,12,512,512]{2,3,1,0:T(8,128)} %get-tuple-element.117, pred[2,512,512]{1,2,0:T(8,128)(4,1)S(1)} %copy-done.6), kind=kLoop, calls=%fused_computation.6 | loop fusion | flops 25153536 | bytes 25788416 | tf_op jit(solution)/shard_map/reduce_sum | solution.py:323
  201.9 12.2 %fusion.23 = bf16[2,512,12,64]{1,3,2,0:T(8,128)(2,1)S(1)} fusion(f32[2,12,512]{2,1,0:T(8,128)S(1)} %fusion, f32[2,12,512]{2,1,0:T(8,128)S(1)} %get-tuple-element.116, f32[2,12,512,512]{2,3,1,0:T(8,128)} %get-tuple-element.117, pred[2,512,512]{1,2,0:T(8,128)(4,1)S(1)} %copy-done.6, bf16[2,512,12,64]{1,0,3,2:T(2,128)(2,1)S(1)} %copy-done.13), kind=kOutput, calls=%fused_computation.71 | convolution fusion | flops 837550080 | bytes 28934144 | tf_op jit(solution)/shard_map/shqk,skhe->sqhe/dot_general | solution.py:326
  218.7 12.0 %multiply_convert_fusion.1 = (bf16[1024,3072]{1,0:T(8,128)(2,1)S(1)}, f32[1024,3072]{1,0:T(8,128)}) fusion(f32[3072]{0:T(1024)S(1)} %copy-done.32, bf16[768,3072]{1,0:T(8,128)(2,1)} %bitcast.171, f32[1024,768]{0,1:T(8,128)S(1)} %get-tuple-element.84, f32[768]{0:T(1024)S(1)} %copy-done.33, f32[768]{0:T(1024)S(1)} %reshape.349, f32[1024]{0:T(1024)S(1)} %fusion.42, ...), kind=kOutput, calls=%fused_computation.14 | convolution fusion | flops 4854644736 | bytes 26765312 | tf_op jit(solution)/shard_map/dot_general | solution.py:337
  230.7 10.4 %fusion.50 = (f32[1024]{0:T(1024)S(1)}, f32[1024,768]{0,1:T(8,128)S(1)}, f32[1024]{0:T(1024)S(1)}) fusion(f32[768]{0:T(1024)S(1)} %copy-done.34, bf16[1024,3072]{1,0:T(8,128)(2,1)S(1)} %get-tuple-element.118, bf16[3072,768]{1,0:T(8,128)(2,1)} %bitcast.175, f32[768]{0:T(1024)S(1)} %copy-done.33, f32[768]{0:T(1024)S(1)} %reshape.349, f32[1024]{0:T(1024)S(1)} %fusion.42, ...), kind=kOutput, calls=%fused_computation.147 | convolution fusion | flops 4842059776 | bytes 17327104 | tf_op jit(solution)/shard_map/dot_general | solution.py:341
  249.8 12.8 %convert_reduce_fusion = (f32[3072]{0:T(1024)S(1)}, bf16[1024,3072]{1,0:T(8,128)(2,1)S(1)}) fusion(bf16[1024,768]{0,1:T(8,128)(2,1)S(1)} %get-tuple-element.76, bf16[3072,768]{1,0:T(8,128)(2,1)} %bitcast.176, f32[1024,3072]{1,0:T(8,128)} %get-tuple-element.119, f32[3072]{0:T(1024)S(1)} %copy-done.32), kind=kOutput, calls=%fused_computation.11 | convolution fusion | flops 4882166784 | bytes 25190400 | tf_op jit(solution)/shard_map/dot_general | solution.py:411
  262.6 7.1 %convolution_convert_fusion = bf16[3072,768]{1,0:T(8,128)(2,1)} fusion(bf16[1024,3072]{1,0:T(8,128)(2,1)S(1)} %bitcast.197, bf16[1024,768]{0,1:T(8,128)(2,1)S(1)} %get-tuple-element.76), kind=kOutput, calls=%fused_computation.19 | convolution fusion | flops 4834197504 | bytes 12582912 | tf_op jit(solution)/shard_map/dot_general | solution.py:410
  269.7 8.4 %multiply_reduce_fusion.5 = (f32[768]{0:T(1024)S(1)}, f32[1024]{0:T(1024)S(1)}, f32[1024]{0:T(1024)S(1)}, f32[768]{0:T(1024)S(1)}, f32[1024,768]{0,1:T(8,128)}) fusion(f32[1024,768]{0,1:T(8,128)S(1)} %copy-done.11, f32[1024]{0:T(1024)S(1)} %fusion.42, f32[1024]{0:T(1024)S(1)} %broadcast_multiply_fusion.1, f32[768]{0:T(1024)S(1)} %reshape.349, ...), kind=kOutput, calls=%fused_computation.44 | convolution fusion | flops 4848349184 | bytes 22065152 | tf_op jit(solution)/shard_map/dot_general | solution.py:416
  278.2 9.2 %copy.132 = bf16[32,2,48,768]{3,1,2,0:T(2,128)(2,1)} copy(bf16[32,2,48,768]{3,2,1,0:T(8,128)(2,1)} %bitcast.177) | data formatting | bytes 9437184 | tf_op jit(solution)/shard_map/reshape | solution.py:682
  287.4 11.6 %concatenate.58 = bf16[4,2,2,2,48,1536]{5,4,3,2,1,0:T(8,128)(2,1)} reshape(bf16[32,48,2,768]{3,2,1,0:T(2,128)(2,1)} %bitcast.157) | data formatting | bytes 9437184 | tf_op jit(solution)/shard_map/concatenate | solution.py:683
  299.1 3.8 fusion.49
  304.6 7.1 %convolution_convert_fusion.1 = bf16[768,3072]{1,0:T(8,128)(2,1)} fusion(bf16[1024,3072]{1,0:T(8,128)(2,1)S(1)} %copy-done.37, f32[1024,768]{0,1:T(8,128)S(1)} %copy-done.12, f32[768]{0:T(1024)S(1)} %copy-done.33, f32[768]{0:T(1024)S(1)} %reshape.349, f32[1024]{0:T(1024)S(1)} %fusion.42, f32[1024]{0:T(1024)S(1)} %broadcast_multiply_fusion.1), kind=kOutput, calls=%fused_computation.20 | convolution fusion | flops 4838129664 | bytes 14170112 | tf_op jit(solution)/shard_map/dot_general | solution.py:415
  311.7 11.6 %reshape.338 = bf16[32,24,2,1536]{3,2,1,0:T(2,128)(2,1)} reshape(bf16[768,3072]{1,0:T(8,128)(2,1)} %convolution_convert_fusion.1) | data formatting | bytes 9437184 | tf_op jit(solution)/shard_map/reshape | solution.py:680
  323.4 5.6 copy.77
  345.4 13.3 %convert_reduce_fusion.4 = (f32[12,64]{1,0:T(8,128)S(1)}, bf16[2,512,12,64]{1,3,2,0:T(8,128)(2,1)}) fusion(f32[2,12,512]{2,1,0:T(8,128)S(1)} %log_add_fusion, f32[2,12,512,512]{2,3,1,0:T(8,128)} %get-tuple-element.117, pred[2,512,512]{1,2,0:T(8,128)(4,1)S(1)} %copy-done.7, bf16[2,512,12,64]{1,0,3,2:T(2,128)(2,1)S(1)} %reshape.333), kind=kOutput, calls=%fused_computation.46 | convolution fusion | flops 832830720 | bytes 28888064 | tf_op jit(solution)/shard_map/shqk,sqhe->skhe/dot_general | solution.py:434
  363.6 18.0 %multiply_reduce_fusion = (f32[2,12,512]{2,1,0:T(8,128)S(1)}, f32[2,12,512,512]{2,3,1,0:T(8,128)}) fusion(f32[2,12,512]{2,1,0:T(8,128)S(1)} %log_add_fusion, f32[2,12,512,512]{2,3,1,0:T(8,128)} %get-tuple-element.117, pred[2,512,512]{1,2,0:T(8,128)(4,1)S(1)} %copy-done.7, bf16[2,512,12,64]{1,0,3,2:T(2,128)(2,1)S(1)} %copy-done.14, ...), kind=kOutput, calls=%fused_computation.1 | convolution fusion | flops 836751360 | bytes 54099968 | tf_op jit(solution)/shard_map/sqhe,skhe->shqk/dot_general | solution.py:431
  381.6 21.6 %multiply_convert_fusion = bf16[2,12,512,512]{2,3,1,0:T(8,128)(2,1)} fusion(f32[2,12,512,512]{2,3,1,0:T(8,128)} %get-tuple-element.122, f32[2,12,512]{2,1,0:T(8,128)S(1)} %get-tuple-element.121, f32[2,12,512]{2,1,0:T(8,128)S(1)} %log_add_fusion, f32[2,12,512,512]{2,3,1,0:T(8,128)} %get-tuple-element.117, pred[2,512,512]{1,2,0:T(8,128)(4,1)S(1)} %copy-done.7), kind=kLoop, calls=%fused_computation | loop fusion | flops 37748736 | bytes 63537152 | tf_op jit(solution)/shard_map/convert_element_type | solution.py:438
  403.2 8.6 %fusion.22 = bf16[2,512,12,64]{1,3,2,0:T(8,128)(2,1)S(1)} fusion(bf16[2,12,512,512]{2,3,1,0:T(8,128)(2,1)} %multiply_convert_fusion, bf16[2,512,12,64]{1,0,3,2:T(2,128)(2,1)S(1)} %copy-done.5), kind=kOutput, calls=%fused_computation.70 | convolution fusion | flops 806879232 | bytes 15728640 | tf_op jit(solution)/shard_map/shqk,sqhe->skhe/dot_general | solution.py:444
  411.8 6.8 %convert_reduce_fusion.5 = (f32[12,64]{1,0:T(8,128)S(1)}, bf16[2,512,12,64]{1,3,2,0:T(8,128)(2,1)S(1)}) fusion(bf16[2,12,512,512]{2,3,1,0:T(8,128)(2,1)} %multiply_convert_fusion, bf16[2,512,12,64]{1,0,3,2:T(2,128)(2,1)S(1)} %copy-done.3), kind=kOutput, calls=%fused_computation.47 | convolution fusion | flops 808451328 | bytes 15731712 | tf_op jit(solution)/shard_map/shqk,skhe->sqhe/dot_general | solution.py:440
  427.6 5.5 add_add_fusion.2
  433.0 5.5 fusion.7
  438.5 4.3 copy.75
  448.5 10.5 %copy_bitcast_fusion.parts_ref = bf16[2,2,2,4,48,4608]{5,4,3,2,1,0:T(8,128)(2,1)} fusion(bf16[4,2,2,2,48,1536]{5,4,3,2,1,0:T(8,128)(2,1)} %concatenate.58, bf16[4,2,2,2,48,1536]{5,4,3,2,1,0:T(8,128)(2,1)} %bitcast.155, bf16[4,2,2,2,48,384]{5,4,3,2,1,0:T(8,128)(2,1)S(1)} %bitcast.185, bf16[4,2,2,2,48,1152]{5,4,3,2,1,0:T(8,128)(2,1)S(1)} %bitcast.161), kind=kLoop, calls=%fused_computation.9 | loop fusion | flops 56623104 | bytes 28311552 | tf_op jit(solution)/shard_map/transpose | solution.py:687
  459.0 103.0 %scatter.1 = (f32[48,4608]{1,0:T(8,128)}, f32[16,768]{1,0:T(8,128)}) custom-call(bf16[2,2,2,4,48,4608]{5,4,3,2,1,0:T(8,128)(2,1)} %copy_bitcast_fusion.parts_ref, f32[16,768]{1,0:T(8,128)} %concatenate.61.small_ref), custom_call_target="tpu_custom_call" | custom-call | tf_op jit(solution)/shard_map/scatter/pallas_call | solution.py:577
  (193 shorter events, 105.0 us)
Async XLA Ops:
  0.6 12.8 %copy-start.20 = (bf16[1024,768]{1,0:T(8,128)(2,1)S(1)}, bf16[1024,768]{1,0:T(8,128)(2,1)}, u32[]{:S(2)}) copy-start(bf16[1024,768]{1,0:T(8,128)(2,1)} %param.33) | copy-start | bytes 4718596
  0.7 14.4 %copy-start.21 = (bf16[1024,768]{1,0:T(8,128)(2,1)S(1)}, bf16[1024,768]{1,0:T(8,128)(2,1)}, u32[]{:S(2)}) copy-start(bf16[1024,768]{1,0:T(8,128)(2,1)} %param.17) | copy-start | bytes 4718596
  119.8 5.2 copy-start
  163.0 4.9 copy-start.17
  171.9 7.1 %copy-start.2 = (bf16[2,512,12,64]{1,0,3,2:T(2,128)(2,1)}, bf16[2,512,12,64]{1,0,3,2:T(2,128)(2,1)S(1)}, u32[]{:S(2)}) copy-start(bf16[2,512,12,64]{1,0,3,2:T(2,128)(2,1)S(1)} %reshape.325) | copy-start | bytes 4718596
  179.0 11.7 %copy-start.4 = (bf16[2,512,12,64]{1,0,3,2:T(2,128)(2,1)}, bf16[2,512,12,64]{1,0,3,2:T(2,128)(2,1)S(1)}, u32[]{:S(2)}) copy-start(bf16[2,512,12,64]{1,0,3,2:T(2,128)(2,1)S(1)} %reshape.324) | copy-start | bytes 4718596
  179.0 11.7 %copy-start.6 = (pred[2,512,512]{1,2,0:T(8,128)(4,1)S(1)}, pred[2,512,512]{1,2,0:T(8,128)(4,1)}, u32[]{:S(2)}) copy-start(pred[2,512,512]{1,2,0:T(8,128)(4,1)} %or_and_fusion) | copy-start | bytes 1572868
  190.7 11.2 %copy-start.13 = (bf16[2,512,12,64]{1,0,3,2:T(2,128)(2,1)S(1)}, bf16[2,512,12,64]{1,0,3,2:T(2,128)(2,1)}, u32[]{:S(2)}) copy-start(bf16[2,512,12,64]{1,0,3,2:T(2,128)(2,1)} %reshape.323) | copy-start | bytes 4718596
  218.0 12.7 %copy-start.10 = (f32[1024,768]{0,1:T(8,128)}, f32[1024,768]{0,1:T(8,128)S(1)}, u32[]{:S(2)}) copy-start(f32[1024,768]{0,1:T(8,128)S(1)} %get-tuple-element.84) | copy-start | bytes 9437188
  218.7 12.0 %copy-start.34 = (f32[768]{0:T(1024)S(1)}, f32[768]{0:T(1024)}, u32[]{:S(2)}) copy-start(f32[768]{0:T(1024)} %reshape.352) | copy-start | bytes 9220
  230.7 10.5 %copy-start.38 = (bf16[1024,3072]{1,0:T(8,128)(2,1)}, bf16[1024,3072]{1,0:T(8,128)(2,1)S(1)}, u32[]{:S(2)}) copy-start(bf16[1024,3072]{1,0:T(8,128)(2,1)S(1)} %get-tuple-element.118) | copy-start | bytes 18874372
  243.9 3.1 copy-start.1
  247.0 15.6 %slice-start.2 = ((s8[6291456]{0:T(1024)(128)(4,1)}), s8[4194304]{0:T(1024)(128)(4,1)S(1)}, s32[]{:S(2)}) async-start(s8[6291456]{0:T(1024)(128)(4,1)} %bitcast.196), calls=%async_computation.2 | async-start | bytes 8388608
  247.0 22.7 %slice-start = ((s8[4718592]{0:T(1024)(128)(4,1)}), s8[4194304]{0:T(1024)(128)(4,1)S(1)}, s32[]{:S(2)}) async-start(s8[4718592]{0:T(1024)(128)(4,1)} %bitcast.172), calls=%async_computation | async-start | bytes 8388608
  249.8 12.8 %slice-start.3 = ((s8[6291456]{0:T(1024)(128)(4,1)}), s8[2097152]{0:T(1024)(128)(4,1)S(1)}, s32[]{:S(2)}) async-start(s8[6291456]{0:T(1024)(128)(4,1)} %bitcast.196), calls=%async_computation.3 | async-start | bytes 4194304
  249.8 19.9 %slice-start.1 = ((s8[4718592]{0:T(1024)(128)(4,1)}), s8[524288]{0:T(1024)(128)(4,1)S(1)}, s32[]{:S(2)}) async-start(s8[4718592]{0:T(1024)(128)(4,1)} %bitcast.172), calls=%async_computation.1 | async-start | bytes 1048576
  262.6 7.1 %copy-start.36 = (bf16[1024,3072]{1,0:T(8,128)(2,1)}, bf16[1024,3072]{1,0:T(8,128)(2,1)S(1)}, u32[]{:S(2)}) copy-start(bf16[1024,3072]{1,0:T(8,128)(2,1)S(1)} %get-tuple-element.128) | copy-start | bytes 18874372
  262.6 7.1 %copy-start.11 = (f32[1024,768]{0,1:T(8,128)S(1)}, f32[1024,768]{0,1:T(8,128)}, u32[]{:S(2)}) copy-start(f32[1024,768]{0,1:T(8,128)} %copy-done.10) | copy-start | bytes 9437188
  299.0 3.8 copy-start.12
  299.1 5.6 copy-start.37
  304.6 30.8 %copy-start.8 = (f32[1024,768]{0,1:T(8,128)}, f32[1024,768]{0,1:T(8,128)S(1)}, u32[]{:S(2)}) copy-start(f32[1024,768]{0,1:T(8,128)S(1)} %get-tuple-element.80) | copy-start | bytes 9437188
  323.4 5.6 copy-start.31
  340.8 4.5 copy-start.7
  345.4 13.3 %copy-start.15 = (bf16[2,512,12,64]{1,0,3,2:T(2,128)(2,1)}, bf16[2,512,12,64]{1,0,3,2:T(2,128)(2,1)S(1)}, u32[]{:S(2)}) copy-start(bf16[2,512,12,64]{1,0,3,2:T(2,128)(2,1)S(1)} %reshape.333) | copy-start | bytes 4718596
  358.7 4.9 copy-start.14
  381.6 21.6 %copy-start.5 = (bf16[2,512,12,64]{1,0,3,2:T(2,128)(2,1)S(1)}, bf16[2,512,12,64]{1,0,3,2:T(2,128)(2,1)}, u32[]{:S(2)}) copy-start(bf16[2,512,12,64]{1,0,3,2:T(2,128)(2,1)} %copy-done.4) | copy-start | bytes 4718596
  403.2 8.6 %copy-start.3 = (bf16[2,512,12,64]{1,0,3,2:T(2,128)(2,1)S(1)}, bf16[2,512,12,64]{1,0,3,2:T(2,128)(2,1)}, u32[]{:S(2)}) copy-start(bf16[2,512,12,64]{1,0,3,2:T(2,128)(2,1)} %copy-done.2) | copy-start | bytes 4718596
  424.1 2.5 copy-start.18
  424.2 3.3 copy-start.9
  427.6 5.5 copy-start.23
  445.9 2.6 copy-start.27
  459.0 106.1 %copy-start.19 = (f32[1024,768]{0,1:T(8,128)S(1)}, f32[1024,768]{0,1:T(8,128)}, u32[]{:S(2)}) copy-start(f32[1024,768]{0,1:T(8,128)} %add_add_fusion.2) | copy-start | bytes 9437188
  (11 other events, 17.0 us)

commit v2 on v0

v2 whole, which is shorter than its diff:
```python
import functools

import jax
import jax.numpy as jnp
from jax import lax
from jax.experimental import pallas as pl
from jax.experimental.pallas import tpu as pltpu
from jax.sharding import PartitionSpec as P

BLOCKS = 32
F32, BF16 = jnp.float32, jnp.bfloat16
LOG2E = 1.4426950408889634
MESH = pl.DeviceIdType.MESH
ALL = slice(None)
ANY = pl.BlockSpec(memory_space=pl.ANY)
VMEM = pl.BlockSpec(memory_space=pltpu.VMEM)
SDS = jax.ShapeDtypeStruct
DMA = pltpu.SemaphoreType.DMA
NT = (((1,), (1,)), ((), ()))
TN = (((0,), (0,)), ((), ()))
NN = (((1,), (0,)), ((), ()))
D, FF, LEN, PAIRS = 768, 3072, 512, 6
ROWS = 256


def tiles_of(counts):
    out, at = [], 0
    for count in counts:
        out.append((at * 128, count * 128))
        at += count
    return tuple(out)


def dot(a, b, dims=NN):
    return lax.dot_general(a, b, dims, preferred_element_type=F32)


def aligned(at, step, size=None):
    return pl.ds(pl.multiple_of(at * step, step), step if size is None else size)


def loop(count, body):
    def step(i, carry):
        body(i)
        return carry

    lax.fori_loop(0, count, step, 0)


def cost(flops, moved, exps=0):
    return pl.CostEstimate(flops=int(flops), bytes_accessed=int(moved), transcendentals=int(exps))


VMEM_LIMIT = 62 * 2**20


class Net:
    def __init__(self, Z, Y):
        self.Z, self.Y = Z, Y
        dp, y = lax.axis_index("dp"), lax.axis_index("fsdp")
        self.fsdp = y
        self.at = {"z": dp // 4, "x": (dp // 2) % 2, "c": dp % 2, "y": y if Y == 2 else 0}
        self.size = {"z": Z, "x": 2, "y": Y}
        self.orders = ["zxy", "xyz", "yzx"] if Y == 2 else ["zx", "xz", "zx"]
        self.own = dp * Y + (y if Y == 2 else 0)

    def device(self, **moved):
        p = dict(self.at, **moved)
        return (p["z"] * 4 + p["x"] * 2 + p["c"], p["y"] if self.Y == 2 else self.fsdp)

    def across(self, axis):
        return self.device(**{axis: 1 - self.at[axis]})

    def barrier(self):
        bar = pltpu.get_barrier_semaphore()
        z, Z = self.at["z"], self.Z
        others = [self.across(axis) for axis in (["c", "x", "y"] if self.Y == 2 else ["c", "x"])]
        others += [self.device(z=(z + k) % Z) for k in range(1, Z)]
        for other in others:
            pl.semaphore_signal(bar, inc=1, device_id=other, device_id_type=MESH)
        pl.semaphore_wait(bar, len(others))

    def place(self, i):
        Y = self.Y
        return ((i // Y) % 2, (i // (2 * Y)) % 2, i % Y, i // (4 * Y))

    def mine(self):
        at = self.at
        return (at["c"], at["x"], at["y"], at["z"])


def sem_count(Z):
    return 18 * (Z - 1) + 3


def sem_at(Z, part, phase, step=0, down=0):
    return ((part * 3 + phase) * 2 + down) * (Z - 1) + step


def remote(src, dst, sems, sem, device):
    return pltpu.make_async_remote_copy(
        src_ref=src,
        dst_ref=dst,
        send_sem=sems[0].at[sem],
        recv_sem=sems[1].at[sem],
        device_id=device,
        device_id_type=MESH,
    )


def gather_chains(net, buf, cols, sems):
    Z, at = net.Z, net.at
    chains = []
    for part, order in enumerate(net.orders):
        col = pl.ds(*cols[part])

        def block(core, idx, col=col):
            return buf.at[core, idx["x"], idx["y"], idx["z"], :, col]

        chain, done = [], set()
        for phase, axis in enumerate(order):
            base = {k: (ALL if k in done else at[k]) for k in "xyz"}
            for step in range(Z - 1 if axis == "z" else 1):
                up_sem, down_sem = (sem_at(Z, part, phase, step, d) for d in (0, 1))

                def swap(axis=axis, base=base, block=block, sem=up_sem):
                    def copy():
                        r = block(at["c"], base)
                        return remote(r, r, sems, sem, net.across(axis))

                    return lambda: copy().start(), lambda: copy().wait_recv(), lambda: copy().wait_send()

                def line(base=base, block=block, step=step, us=up_sem, ds=down_sem):
                    z = at["z"]

                    def copy(from_z, sem, to_z):
                        r = block(at["c"], dict(base, z=from_z))
                        return remote(r, r, sems, sem, net.device(z=to_z))

                    sends = (
                        ((z >= step) & (z + 1 < Z), lambda: copy(z - step, us, z + 1)),
                        ((z + step < Z) & (z > 0), lambda: copy(z + step, ds, z - 1)),
                    )
                    takes = (
                        (z - 1 - step >= 0, lambda: copy(z - 1 - step, us, z - 1)),
                        (z + 1 + step < Z, lambda: copy(z + 1 + step, ds, z + 1)),
                    )

                    def start():
                        for cond, make in sends:
                            pl.when(cond)(lambda make=make: make().start())

                    def receive():
                        for cond, make in takes:
                            pl.when(cond)(lambda make=make: make().wait_recv())

                    def sent():
                        for cond, make in sends:
                            pl.when(cond)(lambda make=make: make().wait_send())

                    return start, receive, sent

                chain.append((phase, line() if axis == "z" else swap()))
            done.add(axis)

        def core(block=block, sem=sem_count(Z) - 3 + part):
            every = {k: ALL for k in "xyz"}

            def copy(c):
                r = block(c, every)
                return remote(r, r, sems, sem, net.across("c"))

            c = at["c"]
            return lambda: copy(c).start(), lambda: copy(1 - c).wait_recv(), lambda: copy(c).wait_send()

        chain.append((len(order), core()))
        chains.append(chain)
    return chains


def add_into(dst, src, lead):
    total = 1
    for n in lead:
        total *= n

    def one(i):
        idx = []
        for n in reversed(lead):
            idx.append(i % n)
            i = i // n
        idx = tuple(reversed(idx))
        dst[idx] = (dst[idx].astype(F32) + src[idx].astype(F32)).astype(dst.dtype)

    if total == 1:
        one(0)
    else:
        loop(total, one)


def scatter_scratch(net_sizes, cols, rows=48):
    Z, Y = net_sizes
    size = {"x": 2, "y": Y, "z": Z}
    orders = ["zxy", "xyz", "yzx"] if Y == 2 else ["zx", "xz", "zx"]
    out = []
    for part, order in enumerate(orders):
        width = cols[part][1]
        free = list(order)
        out.append(pltpu.VMEM(tuple(size[k] for k in "xyz" if k in free) + (rows, width), BF16))
        for axis in reversed(order):
            free.remove(axis)
            lead = tuple(size[k] for k in "xyz" if k in free)
            if axis == "z":
                lead = (2, Z - 1) + lead
            out.append(pltpu.VMEM(lead + (rows, width), BF16))
    return out


def scatter_chains(net, buf, cols, scratch, sems):
    Z, at = net.Z, net.at
    scratch = list(scratch)
    chains = []
    for part, order in enumerate(net.orders):
        col = pl.ds(*cols[part])
        arrive = [scratch.pop(0) for _ in range(len(order) + 1)]

        def block(core, idx, col=col):
            return buf.at[core, idx["x"], idx.get("y", 0), idx["z"], :, col]

        def lead_of(free):
            return tuple(net.size[k] for k in "xyz" if k in free)

        def swap(send, keep, land, sem, device, lead):
            def copy():
                return remote(send(), land, sems, sem, device())

            def receive():
                copy().wait_recv()
                add_into(keep(), land, lead)

            return lambda: copy().start(), receive, lambda: copy().wait_send()

        every = {k: ALL for k in order}
        chain = [
            (
                0,
                swap(
                    lambda block=block, every=every: block(1 - at["c"], every),
                    lambda block=block, every=every: block(at["c"], every),
                    arrive[0],
                    sem_count(Z) - 3 + part,
                    lambda: net.across("c"),
                    lead_of(order),
                ),
            )
        ]
        free = list(order)
        for phase, axis in enumerate(reversed(order)):
            free.remove(axis)
            base = {k: (ALL if k in free else at[k]) for k in order}
            land, lead = arrive[1 + phase], lead_of(free)
            if axis != "z":
                chain.append(
                    (
                        phase + 1,
                        swap(
                            lambda block=block, base=base, axis=axis: block(at["c"], dict(base, **{axis: 1 - at[axis]})),
                            lambda block=block, base=base, axis=axis: block(at["c"], dict(base, **{axis: at[axis]})),
                            land,
                            sem_at(Z, part, phase),
                            lambda axis=axis: net.across(axis),
                            lead,
                        ),
                    )
                )
                continue
            for step in range(Z - 1):
                us, ds = (sem_at(Z, part, phase, step, d) for d in (0, 1))

                def line(base=base, block=block, step=step, us=us, ds=ds, land=land, lead=lead):
                    z = at["z"]
                    zr = Z - 1 - z

                    def copy(d, way, sem, to_z):
                        return remote(block(at["c"], dict(base, z=d)), land.at[way, step], sems, sem, net.device(z=to_z))

                    sends = (
                        ((z <= step) & (z < Z - 1), lambda: copy(Z - 1 - step + z, 0, us, z + 1)),
                        ((zr <= step) & (z > 0), lambda: copy(step - zr, 1, ds, z - 1)),
                    )
                    takes = (
                        ((z - 1 <= step) & (z > 0), lambda: copy(z, 0, us, z - 1), Z - 2 - step + z, 0),
                        ((zr - 1 <= step) & (zr > 0), lambda: copy(z, 1, ds, z + 1), step + 1 - zr, 1),
                    )

                    def start():
                        for cond, make in sends:
                            pl.when(cond)(lambda make=make: make().start())

                    def receive():
                        for cond, make, d, way in takes:

                            @pl.when(cond)
                            def _(make=make, d=d, way=way):
                                make().wait_recv()
                                add_into(block(at["c"], dict(base, z=d)), land.at[way, step], lead)

                    def sent():
                        for cond, make in sends:
                            pl.when(cond)(lambda make=make: make().wait_send())

                    return start, receive, sent

                chain.append((phase + 1, line()))
        chains.append(chain)
    return chains


def phased(chains):
    calls, pending = [], [None] * len(chains)
    for phase in range(1 + max(ph for chain in chains for ph, _ in chain)):
        subs = [[step for ph, step in chain if ph == phase] for chain in chains]
        for k in range(max(len(sub) for sub in subs)):
            todo = []
            for j, sub in enumerate(subs):
                if k < len(sub):
                    if pending[j] is not None:
                        todo.append(pending[j])
                    todo.append(sub[k][0])
                    pending[j] = sub[k][1]
            calls.append(todo)
    calls.append([p for p in pending if p is not None])
    return [lambda todo=todo: [call() for call in todo] and None for todo in calls]


def eager(chains):
    calls = []
    for k in range(1 + max(map(len, chains))):
        todo = []
        for chain in chains:
            if 0 < k <= len(chain):
                todo.append(chain[k - 1][1][1])
            if k < len(chain):
                todo.append(chain[k][1][0])
        calls.append(todo)
    return [lambda todo=todo: [call() for call in todo] and None for todo in calls]


def finish(chains):
    for chain in chains:
        for _, step in chain:
            step[2]()


def spread(i, first, calls, every=1):
    for k, call in enumerate(calls):
        pl.when(i == first + k * every)(call)


def head_mask(head, shape):
    lane = lax.broadcasted_iota(jnp.int32, shape, len(shape) - 1)
    return (lane < 64) if head == 0 else (lane >= 64)


def column(row, count=128):
    return jnp.broadcast_to(row, (count, row.shape[1])).T


def build_mask(mask, down, across):
    n = mask.shape[0]
    down = column(down)
    at = lax.broadcasted_iota(jnp.int32, (n, 128), 0)
    lane = lax.broadcasted_iota(jnp.int32, (n, 128), 1)
    for j in range(n // 128):
        tile = slice(j * 128, (j + 1) * 128)
        mask[:, tile] = jnp.where((down == across[:, tile]) | (at == lane + j * 128), 0.0, -1e30)


def gelu_pair(h):
    t = 1.0 / (1.0 + (0.3275911 * 0.7071067811865476) * jnp.abs(h))
    e = jnp.exp2(h * h * (-0.5 * LOG2E))
    poly = t * (
        0.5 * 0.254829592
        + t * (0.5 * -0.284496736 + t * (0.5 * 1.421413741 + t * (0.5 * -1.453152027 + t * (0.5 * 1.061405429))))
    )
    tail = poly * e
    cdf = jnp.where(h >= 0, 1.0 - tail, tail)
    return h * cdf, cdf + h * e * 0.3989422804014327


def normalise(v):
    centred = v - jnp.sum(v, axis=1, keepdims=True) * (1.0 / D)
    r = lax.rsqrt(jnp.sum(centred * centred, axis=1, keepdims=True) * (1.0 / D) + 1e-12)
    return centred * r, r


def norm_back(g, n, r, gain):
    scaled = g * gain
    mean = jnp.sum(scaled, axis=1, keepdims=True) * (1.0 / D)
    along = jnp.sum(scaled * n, axis=1, keepdims=True) * (1.0 / D)
    return r * (scaled - mean - n * along)


def down_sum(v):
    return jnp.sum(v, axis=0, keepdims=True)


def square_sum(value, counted):
    v = value.astype(BF16).astype(F32)
    v = v * v
    total = v[:, :128]
    for j in range(1, D // 128):
        total = total + v[:, j * 128 : (j + 1) * 128]
    return down_sum(total * counted)


def fold_own(shard, half):
    v = shard.astype(F32)
    return jnp.concatenate([v[:, :half], v[:, half:]], axis=0).astype(BF16)


def unfold(net, buf, first, half, dst):
    def pair(p):
        cols = slice(first, first + half)
        a = buf[net.place(2 * p) + (ALL, cols)].astype(F32)
        b = buf[net.place(2 * p + 1) + (ALL, cols)].astype(F32)
        rows = aligned(p, 48)
        dst[rows, :half] = jnp.concatenate([a[:24], b[:24]], axis=0).astype(BF16)
        dst[rows, half:] = jnp.concatenate([a[24:], b[24:]], axis=0).astype(BF16)

    loop(BLOCKS // 2, pair)


PLACES = {"qb": (1, 0), "vb": (1, 1), "ob": (1, 2), "fg": (1, 3), "fs": (2, 0), "sb": (2, 1), "sg": (2, 2), "ss": (2, 3)}


def add_small(small, name, value):
    row, at = PLACES[name]
    small[row : row + 1, at * D : (at + 1) * D] += value


def small_window(net, vectors, expand, tmp):
    tmp[...] = jnp.zeros_like(tmp)
    for k, ref in enumerate(vectors):
        tmp[k : k + 1, : 24] = ref[...].astype(F32)
    tmp[8:9, : 96] = expand[...].astype(F32)
    i = net.own
    v = pltpu.roll(tmp[0:8, :], (24 * i) % 128, axis=1)
    e = pltpu.roll(tmp[8:16, :], (96 * i) % 128, axis=1)
    both = jnp.concatenate([v, e], axis=0)
    return jnp.concatenate([both[:, :128], both[:, 128:]], axis=0).astype(BF16)


def small_params(net, buf, first, vec, exp):
    vec[...] = jnp.zeros_like(vec)
    exp[...] = jnp.zeros_like(exp)
    for i in range(BLOCKS):
        w = buf[net.place(i) + (slice(0, 32), slice(first, first + 128))].astype(F32)
        for ref, rows, tile in ((vec, 0, 24 * i // 128), (exp, 8, 96 * i // 128)):
            for k in range(2):
                if (tile + k) * 128 < ref.shape[1]:
                    ref[:, (tile + k) * 128 : (tile + k + 1) * 128] += w[16 * k + rows : 16 * k + rows + 8]


def project(x, w, vec, qkv):
    def body(i):
        r = aligned(i, ROWS)
        xv = x[r, :]
        for j in range(3):
            c = dot(xv, w[:, j * D : (j + 1) * D])
            if j != 1:
                c = c + vec[j // 2 : j // 2 + 1, :]
            c = c.astype(BF16)
            for p in range(PAIRS):
                qkv[j * PAIRS + p, r, :] = c[:, p * 128 : (p + 1) * 128]

    return body


def attend(qkv, mask, att, lse, seq, p):
    base = pl.multiple_of(seq * LEN, LEN)
    q, k, v = (qkv[j * PAIRS + p, pl.ds(base, LEN), :] for j in range(3))
    lane = lax.broadcasted_iota(jnp.int32, (LEN, 128), 1)
    out, logs = None, lse[pl.ds(base, LEN), :]
    for head in range(2):
        here = head_mask(head, k.shape)
        km, vm = jnp.where(here, k, jnp.zeros_like(k)), jnp.where(here, v, jnp.zeros_like(v))
        t = dot(q, km, NT) * (0.125 * LOG2E) + mask[seq]
        top = jnp.max(t, axis=1, keepdims=True)
        e = jnp.exp2(t - top)
        total = jnp.sum(e, axis=1, keepdims=True)
        o = dot(e.astype(BF16), vm) * (1.0 / total)
        out = o if out is None else out + o
        logs = jnp.where(lane == 2 * p + head, top + jnp.log2(total), logs)
    lse[pl.ds(base, LEN), :] = logs
    att[pl.ds(base, LEN), aligned(p, 128)] = out.astype(BF16)


def forward_kernel(Z, Y, groups, *refs):
    (x_h, cot_h, codes, w_in_s, w_out_s, w1_s, w2_s, qb, vb, ob, fg, fs, eb, sb, sg, ss_) = refs[:16]
    (res_h, qkv_h, att_h, normed_h, act_h, gp_h, df_h, lse_h, w_in_h, w_out_h, w1_h, w2_h, result_h, dsec_h, vec, small) = refs[16:32]
    (g1, g2, g3, w_in, w_out, w1, w2, x, qkv, mask, att, lse, lse_rows, wide, normed, act, gp, cot, exp, tmp, s1, r1, s2, r2, s3, r3, loads, outs, gsem) = refs[32:]
    net = Net(Z, Y)
    T = x.shape[0]
    seqs = T // LEN
    blocks = T // ROWS

    load_x = pltpu.make_async_copy(x_h, x, loads.at[0])
    load_x.start()
    load_cot = pltpu.make_async_copy(cot_h, cot, loads.at[1])
    load_cot.start()
    mine = net.mine()
    g1[mine + (ALL, slice(0, 1152))] = fold_own(w_in_s[...], 1152)
    g1[mine + (slice(0, 32), slice(1152, 1280))] = small_window(net, (qb, vb, ob, fg, fs, sb, sg, ss_), eb, tmp)
    g1[mine + (slice(32, 48), slice(1152, 1280))] = jnp.zeros((16, 128), BF16)
    net.barrier()
    chains = [gather_chains(net, g, cols, s) for g, cols, s in zip((g1, g2, g3), groups, ((s1, r1), (s2, r2), (s3, r3)))]
    first = eager(chains[0])
    first[0]()
    g2[mine + (ALL, slice(0, 384))] = fold_own(w_out_s[...], 384)
    g2[mine + (ALL, slice(384, 1920))] = fold_own(w1_s[...], 1536)
    g3[mine + (ALL, slice(0, D))] = w2_s[0:48, :]
    g3[mine + (ALL, slice(D, 2 * D))] = w2_s[48:96, :]
    small[...] = jnp.zeros_like(small)
    for s in range(seqs):
        build_mask(mask.at[s], codes[s, 0:1, :], codes[s, 1:2, :])
        valid = codes[s, 2:3, :]
        small[3:4, 512:640] += sum(valid[:, j * 128 : (j + 1) * 128] for j in range(LEN // 128))
    lse[...] = jnp.zeros_like(lse)
    for call in first[1:]:
        call()
    calls = phased(chains[1]) + phased(chains[2])
    n2 = len(phased(chains[1]))
    calls[0]()
    unfold(net, g1, 0, 1152, w_in)
    small_params(net, g1, 1152, vec, exp)
    load_x.wait()
    do_project = project(x, w_in, vec, qkv)

    def project_step(i):
        spread(i, 1, calls[1:4])
        do_project(i)

    loop(blocks, project_step)
    stores = []

    def store(src, dst):
        copy = pltpu.make_async_copy(src, dst, outs.at[len(stores)])
        copy.start()
        stores.append(copy)
        return copy

    store(qkv, qkv_h)
    store(w_in, w_in_h)

    def attend_step(i):
        spread(i, 1, calls[4 : n2 + 2], 1)
        attend(qkv, mask, att, lse, i // PAIRS, i % PAIRS)

    loop(seqs * PAIRS, attend_step)
    store_att = store(att, att_h)
    for s in range(seqs):
        rows = lse[s * LEN : (s + 1) * LEN, :].T
        for h in range(2 * PAIRS):
            lse_rows[s * 2 * PAIRS + h] = jnp.broadcast_to(rows[h : h + 1, :], (8, LEN))
    store(lse_rows, lse_h)
    unfold(net, g2, 0, 384, w_out)
    unfold(net, g2, 384, 1536, w1)
    store(w_out, w_out_h)
    store(w1, w1_h)

    def counted(i):
        per = LEN // ROWS
        return column(codes[i // per, 2:3, aligned(i % per, ROWS)])

    def out_step(i):
        spread(i, 0, calls[n2 + 2 : n2 + 6])
        r = aligned(i, ROWS)
        branch = dot(att[r, :], w_out[...]) + vec[2:3, :]
        residual = x[r, :].astype(F32) + branch
        wide[r, :] = residual
        n, _ = normalise(residual)
        normed[r, :] = (n * vec[3:4, :] + vec[4:5, :]).astype(BF16)
        live = counted(i)
        small[3:4, 0:128] += square_sum(residual, live)
        small[3:4, 128:256] += square_sum(branch, live)

    loop(blocks, out_step)
    store_wide = store(wide, res_h)
    store(normed, normed_h)

    def gp_copy(i):
        return pltpu.make_async_copy(gp.at[i % 2], gp_h.at[aligned(i, ROWS), :], gsem.at[i % 2])

    def expand_step(i):
        spread(i, 0, calls[n2 + 6 : n2 + 10])
        pl.when(i >= 2)(lambda: gp_copy(i).wait())
        r = aligned(i, ROWS)
        nv = normed[r, :]
        for j in range(FF // 512):
            c = slice(j * 512, (j + 1) * 512)
            a, g = gelu_pair(dot(nv, w1[:, c]) + exp[0:1, c])
            act[r, c] = a.astype(BF16)
            gp[i % 2, :, c] = g.astype(BF16)
        gp_copy(i).start()

    loop(blocks, expand_step)
    store(act, act_h)
    for call in calls[n2 + 10 :]:
        call()

    def unfold_last(i):
        blk = g3.at[net.place(i)]
        w2[aligned(i, 96, 48), :] = blk[:, :D]
        w2[pl.ds(pl.multiple_of(i * 96 + 48, 48), 48), :] = blk[:, D:]

    loop(BLOCKS, unfold_last)
    store(w2, w2_h)
    store_wide.wait()
    store_att.wait()
    load_cot.wait()

    def last_step(i):
        r = aligned(i, ROWS)
        feedfwd = dot(act[r, :], w2[...]) + vec[5:6, :]
        second = normed[r, :].astype(F32) + feedfwd
        n, rs = normalise(second)
        gain = vec[6:7, :]
        att[r, :] = (n * gain + vec[7:8, :]).astype(BF16)
        g = cot[r, :].astype(F32)
        grad = norm_back(g, n, rs, gain)
        wide[r, :] = grad
        low = grad.astype(BF16)
        x[r, :] = low
        add_small(small, "sg", down_sum(g * n))
        add_small(small, "ss", down_sum(g))
        add_small(small, "sb", down_sum(low.astype(F32)))
        live = counted(i)
        small[3:4, 256:384] += square_sum(second, live)
        small[3:4, 384:512] += square_sum(feedfwd, live)

    loop(blocks, last_step)
    stores = [copy for copy in stores if copy is not store_wide and copy is not store_att]
    ends = [
        pltpu.make_async_copy(wide, dsec_h, loads.at[0]),
        pltpu.make_async_copy(att, result_h, loads.at[1]),
        pltpu.make_async_copy(x, df_h, loads.at[2]),
    ]
    for copy in ends:
        copy.start()
    for k in (0, 1):
        gp_copy(blocks - 2 + k).wait()
    for copy in stores + ends:
        copy.wait()
    for chain in chains:
        finish(chain)


def forward(Z, Y, x, cot, codes, shards, vectors):
    T, S = x.shape[0], codes.shape[0]
    w_in_s, w_out_s, w1_s, w2_s = shards
    groups = (tiles_of((4, 2, 4)), tiles_of((6, 4, 5)), tiles_of((5, 3, 4)))
    blocks = (2, 2, Y, Z, 48)
    outs = [
        SDS((T, D), F32), SDS((3 * PAIRS, T, 128), BF16), SDS((T, D), BF16), SDS((T, D), BF16),
        SDS((T, FF), BF16), SDS((T, FF), BF16), SDS((T, D), BF16), SDS((S * 12, 8, LEN), F32),
        SDS((D, 3 * D), BF16), SDS((D, D), BF16), SDS((D, FF), BF16), SDS((FF, D), BF16),
        SDS((T, D), BF16), SDS((T, D), F32), SDS((8, D), F32), SDS((8, FF), F32),
    ]
    scratch = [
        pltpu.VMEM(blocks + (1280,), BF16), pltpu.VMEM(blocks + (1920,), BF16), pltpu.VMEM(blocks + (1536,), BF16),
        pltpu.VMEM((D, 3 * D), BF16), pltpu.VMEM((D, D), BF16), pltpu.VMEM((D, FF), BF16), pltpu.VMEM((FF, D), BF16),
        pltpu.VMEM((T, D), BF16), pltpu.VMEM((3 * PAIRS, T, 128), BF16), pltpu.VMEM((S, LEN, LEN), F32),
        pltpu.VMEM((T, D), BF16), pltpu.VMEM((T, 128), F32), pltpu.VMEM((S * 12, 8, LEN), F32),
        pltpu.VMEM((T, D), F32), pltpu.VMEM((T, D), BF16), pltpu.VMEM((T, FF), BF16), pltpu.VMEM((2, ROWS, FF), BF16),
        pltpu.VMEM((T, D), BF16), pltpu.VMEM((8, FF), F32), pltpu.VMEM((16, 256), F32),
    ] + [DMA((sem_count(Z),))] * 6 + [DMA((3,)), DMA((16,)), DMA((2,))]
    return pl.pallas_call(
        functools.partial(forward_kernel, Z, Y, groups),
        out_shape=outs,
        in_specs=[ANY, ANY] + [VMEM] * 14,
        out_specs=[ANY] * 14 + [VMEM] * 2,
        scratch_shapes=scratch,
        compiler_params=pltpu.CompilerParams(collective_id=0, has_side_effects=True, vmem_limit_bytes=VMEM_LIMIT),
        name="forward",
    )(x, cot, codes, w_in_s, w_out_s, w1_s, w2_s, *vectors)


def pack(net, buf, cols, left, right):
    def owner(i):
        rows = aligned(i, 24)
        v = jnp.concatenate([left[rows, :], right[rows, :]], axis=0).astype(BF16)
        buf[net.place(i) + (ALL, cols)] = v

    loop(BLOCKS, owner)


def feed_back_kernel(Z, Y, cols, *refs):
    (act_h, gp_h, df_h, dsec_h, normed_h, res_h, att_h, w1_h, w2_h, w_out_h, vec, small_in) = refs[:12]
    (p1_h, po_h, do_h, dres_h, w2_own, small) = refs[12:18]
    (df, wide, normed, normed_t, att, res, w1, w2, w_out, act, gp, dh, dw, p1, po, p2, ss, rs, loads, chunks, outs) = refs[18:39]
    scratch = refs[39:]
    net = Net(Z, Y)
    T = df.shape[0]
    blocks = T // ROWS

    def load(src, dst, k):
        copy = pltpu.make_async_copy(src, dst, loads.at[k])
        copy.start()
        return copy

    def act_copy(j):
        return pltpu.make_async_copy(act_h.at[:, aligned(j, 384)], act.at[j % 2], chunks.at[j % 2])

    def gp_copies(j):
        return [
            pltpu.make_async_copy(
                gp_h.at[:, pl.ds(pl.multiple_of(side * 1536 + j * 384, 128), 384)],
                gp.at[j % 2, side],
                chunks.at[2 + 2 * side + j % 2],
            )
            for side in range(2)
        ]

    act_copy(0).start()
    load_df = load(df_h, df, 0)
    act_copy(1).start()
    load_w2 = load(w2_h, w2, 1)
    load_normed = load(normed_h, normed, 2)
    for j in range(2):
        for copy in gp_copies(j):
            copy.start()
    load_w1 = load(w1_h, w1, 3)
    load_dsec = load(dsec_h, wide, 4)
    load_rest = [load(res_h, res, 5), load(att_h, att, 6), load(w_out_h, w_out, 7)]
    small[...] = small_in[...]
    net.barrier()
    load_df.wait()

    def shrink_step(j):
        act_copy(j).wait()
        v = dot(act[j % 2], df[...], TN).astype(BF16)
        for k in range(4):
            place = net.place(4 * j + k)
            p2[place + (ALL, slice(0, D))] = v[96 * k : 96 * k + 48]
            p2[place + (ALL, slice(D, 2 * D))] = v[96 * k + 48 : 96 * k + 96]
        pl.when(j + 2 < FF // 384)(lambda: act_copy(j + 2).start())

    loop(FF // 384, shrink_step)
    chains = scatter_chains(net, p2, cols, scratch, (ss, rs))
    calls = phased(chains)
    calls[0]()
    load_normed.wait()

    def turn(j):
        lanes = aligned(j, 128)
        normed_t[lanes, :] = normed[:, lanes].T

    loop(D // 128, turn)
    load_w2.wait()
    load_w1.wait()
    load_dsec.wait()
    points = calls[1:]

    def expand_step(j):
        for copy in gp_copies(j):
            copy.wait()
        for side in range(2):
            spread(j, 0, points[side::3])
            c = pl.ds(pl.multiple_of(side * 1536 + j * 384, 128), 384)
            for i in range(blocks // 2):
                r = slice(i * 2 * ROWS, (i + 1) * 2 * ROWS)
                d = (dot(df[r, :], w2[c, :], NT) * gp[j % 2, side, r, :].astype(F32)).astype(BF16)
                dh[r, side * 384 : side * 384 + 384] = d
                wide[r, :] += dot(d, w1[:, c], NT)
            small[0:1, c] += down_sum(dh[:, side * 384 : side * 384 + 384].astype(F32))
        spread(j, 0, points[2::3])

        @pl.when(j + 2 < 4)
        def _():
            for copy in gp_copies(j + 2):
                copy.start()

        dw[...] = dot(normed_t[...], dh[...])
        pack(net, p1, aligned(j, 384), dw.at[:, :384], dw.at[:, 384:])

    loop(4, expand_step)
    store_p1 = pltpu.make_async_copy(p1, p1_h, outs.at[0])
    store_p1.start()
    for copy in load_rest:
        copy.wait()
    late = points[12:]

    def norm_step(i):
        spread(i, 0, late[:4])
        r = aligned(i, ROWS)
        n, rsd = normalise(res[r, :])
        g = wide[r, :]
        grad = norm_back(g, n, rsd, vec[3:4, :])
        wide[r, :] = grad
        low = grad.astype(BF16)
        df[r, :] = low
        add_small(small, "fg", down_sum(g * n))
        add_small(small, "fs", down_sum(g))
        add_small(small, "ob", down_sum(low.astype(F32)))
        normed[r, :] = dot(low, w_out[...], NT).astype(BF16)

    loop(blocks, norm_step)
    stores = [store_p1, pltpu.make_async_copy(wide, dres_h, outs.at[1]), pltpu.make_async_copy(normed, do_h, outs.at[2])]
    for copy in stores[1:]:
        copy.start()
    for call in late[4:6]:
        call()
    dw[...] = dot(att[...], df[...], TN)
    pack(net, po, ALL, dw.at[:, :384], dw.at[:, 384:])
    stores.append(pltpu.make_async_copy(po, po_h, outs.at[3]))
    stores[-1].start()
    for call in late[6:]:
        call()
    own = p2[net.mine()]
    w2_own[0:48, :] = own[:, :D].astype(F32)
    w2_own[48:96, :] = own[:, D:].astype(F32)
    for copy in stores:
        copy.wait()
    finish(chains)


def feed_back(Z, Y, act, gp, df, dsec, normed, res, att, w1, w2, w_out, vec, small):
    T = df.shape[0]
    cols = tiles_of((5, 3, 4))
    blocks = (2, 2, Y, Z, 48)
    outs = [
        SDS(blocks + (1536,), BF16), SDS(blocks + (384,), BF16), SDS((T, D), BF16), SDS((T, D), F32),
        SDS((96, D), F32), SDS((8, FF), F32),
    ]
    rows = pltpu.VMEM((T, D), BF16)
    scratch = [
        rows, pltpu.VMEM((T, D), F32), rows, pltpu.VMEM((D, T), BF16), rows, pltpu.VMEM((T, D), F32),
        pltpu.VMEM((D, FF), BF16), pltpu.VMEM((FF, D), BF16), pltpu.VMEM((D, D), BF16),
        pltpu.VMEM((2, T, 384), BF16), pltpu.VMEM((2, 2, T, 384), BF16), rows, pltpu.VMEM((D, D), F32),
        pltpu.VMEM(blocks + (1536,), BF16), pltpu.VMEM(blocks + (384,), BF16), pltpu.VMEM(blocks + (1536,), BF16),
        DMA((sem_count(Z),)), DMA((sem_count(Z),)), DMA((8,)), DMA((6,)), DMA((4,)),
    ] + scatter_scratch((Z, Y), cols)
    return pl.pallas_call(
        functools.partial(feed_back_kernel, Z, Y, cols),
        out_shape=outs,
        in_specs=[ANY] * 10 + [VMEM] * 2,
        out_specs=[ANY] * 4 + [VMEM] * 2,
        scratch_shapes=scratch,
        compiler_params=pltpu.CompilerParams(collective_id=1, has_side_effects=True, vmem_limit_bytes=VMEM_LIMIT),
        name="feed_back",
    )(act, gp, df, dsec, normed, res, att, w1, w2, w_out, vec, small)


def attend_back(qkv, do, mask_t, lse, d, small, seq, p):
    base = pl.multiple_of(seq * LEN, LEN)
    rows = pl.ds(base, LEN)
    lanes = aligned(p, 128)
    q, k, v = (qkv[j * PAIRS + p, rows, :] for j in range(3))
    g = do[rows, lanes]
    kt = k.T
    dk = dv = None
    dqt = []
    for h in range(2):
        here = head_mask(h, k.shape)
        km, vm, qm, gm = (jnp.where(here, a, jnp.zeros_like(a)) for a in (k, v, q, g))
        t = dot(km, q, NT) * (0.125 * LOG2E) + mask_t[seq] - lse[seq * 2 * PAIRS + 2 * p + h, 0:1, :]
        pt = jnp.exp2(t)
        dp = dot(vm, g, NT)
        w = pt * dp
        ds = (w - pt * jnp.sum(w, axis=0, keepdims=True)).astype(BF16)
        dvh = dot(pt.astype(BF16), gm)
        dkh = dot(ds, qm)
        dv = dvh if dv is None else dv + dvh
        dk = dkh if dk is None else dk + dkh
        dqt.append(dot(kt[64 * h : 64 * h + 64, :], ds))
    dq = (jnp.concatenate(dqt, axis=0).T * 0.125).astype(BF16)
    dv = dv.astype(BF16)
    d[rows, lanes] = dq
    d[rows, pl.ds(pl.multiple_of(D + p * 128, 128), 128)] = (dk * 0.125).astype(BF16)
    d[rows, pl.ds(pl.multiple_of(2 * D + p * 128, 128), 128)] = dv
    small[1:2, lanes] += down_sum(dq.astype(F32))
    small[1:2, pl.ds(pl.multiple_of(D + p * 128, 128), 128)] += down_sum(dv.astype(F32))


def small_partners(net):
    out = [lambda: net.across("c"), lambda: net.across("x")]
    if net.Y == 2:
        out.append(lambda: net.across("y"))
    bit = 1
    while bit < net.Z:
        def partner(bit=bit):
            z = net.at["z"]
            return net.device(z=z + bit - 2 * bit * ((z // bit) % 2))

        out.append(partner)
        bit *= 2
    return out


def attend_back_kernel(Z, Y, cols, *refs):
    (qkv_h, do_h, x_h, w_in_h, dres_h, p1_h, po_h, codes, lse, small_in) = refs[:10]
    dx_h, w_in_own, w_out_own, w1_own, stats, exp_own = refs[10:16]
    vectors = refs[16:24]
    (qkv, do, d, x, x_t, w_in, wide, mask_t, dw, g2, g1, mine, theirs, edge, s2, r2, s1, r1, sss, srs, loads, outs) = refs[24:46]
    scratch = refs[46:]
    half = len(scratch) // 2
    net = Net(Z, Y)
    T = x.shape[0]
    seqs, blocks = T // LEN, T // ROWS

    def load(src, dst, k):
        copy = pltpu.make_async_copy(src, dst, loads.at[k])
        copy.start()
        return copy

    load_parts = [load(p1_h, g2.at[:, :, :, :, :, pl.ds(384, 1536)], 0), load(po_h, g2.at[:, :, :, :, :, pl.ds(0, 384)], 1)]
    load_heads = [load(qkv_h, qkv, 2), load(do_h, do, 3)]
    load_x = load(x_h, x, 4)
    load_rest = [load(w_in_h, w_in, 5), load(dres_h, wide, 6)]
    small = mine.at[0]
    small[...] = small_in[...]
    net.barrier()
    for copy in load_parts:
        copy.wait()
    chains2 = scatter_chains(net, g2, cols[0], scratch[:half], (s2, r2))
    chains1 = scatter_chains(net, g1, cols[1], scratch[half:], (s1, r1))
    calls = phased(chains2)
    calls[0]()
    for s in range(seqs):
        build_mask(mask_t.at[s], codes[s, 1:2, :], codes[s, 0:1, :])
    load_x.wait()

    def turn(j):
        lanes = aligned(j, 128)
        x_t[lanes, :] = x[:, lanes].T

    loop(D // 128, turn)
    for copy in load_heads:
        copy.wait()

    def attend_step(i):
        spread(i, 0, calls[1:])
        attend_back(qkv, do, mask_t, lse, d, small, i // PAIRS, i % PAIRS)

    loop(seqs * PAIRS, attend_step)
    own2 = g2[net.mine()].astype(F32)
    w_out_own[...] = jnp.concatenate([own2[:24, :384], own2[24:, :384]], axis=1)
    w1_own[...] = jnp.concatenate([own2[:24, 384:], own2[24:, 384:]], axis=1)

    def weight_step(j):
        left = pl.ds(pl.multiple_of(j * 384, 128), 384)
        right = pl.ds(pl.multiple_of(1152 + j * 384, 128), 384)
        dw[:, :384] = dot(x_t[...], d[:, left])
        dw[:, 384:] = dot(x_t[...], d[:, right])
        pack(net, g1, aligned(j, 384), dw.at[:, :384], dw.at[:, 384:])

    loop(3, weight_step)
    calls = eager(chains1)
    partners = small_partners(net)
    sums = [
        remote(mine.at[k], theirs.at[k], (sss, srs), k, partner()) for k, partner in enumerate(partners)
    ]

    def small_call(k):
        if 0 < k <= len(sums):
            sums[k - 1].wait_recv()
            mine[k] = mine[k - 1] + theirs[k - 1]
        if k < len(sums):
            sums[k].start()

    calls = [lambda k=k, call=call: (call(), small_call(k)) and None for k, call in enumerate(calls)]
    assert len(calls) > len(sums)
    calls[0]()
    for copy in load_rest:
        copy.wait()

    def token_step(i):
        spread(i, 0, calls[1:5])
        r = aligned(i, ROWS)
        wide[r, :] += dot(d[r, :], w_in[...], NT)

    loop(blocks, token_step)
    store = pltpu.make_async_copy(wide, dx_h, outs.at[0])
    store.start()
    for call in calls[5:]:
        call()
    own1 = g1[net.mine()].astype(F32)
    w_in_own[...] = jnp.concatenate([own1[:24], own1[24:]], axis=1)
    total = mine[len(sums)]
    edge[:, FF:] = jnp.zeros((8, 128), F32)
    edge[:, :FF] = total
    lane = lax.broadcasted_iota(jnp.int32, (1, 128), 1)
    packed = jnp.zeros((1, 128), F32)
    for k in range(5):
        packed = jnp.where(lane == k, jnp.sum(total[3:4, k * 128 : (k + 1) * 128], axis=1, keepdims=True), packed)
    stats[...] = packed

    def window(at):
        tile = at // 128
        return pltpu.roll(edge[:, pl.ds(pl.multiple_of(tile * 128, 128), 256)], (256 - at % 128) % 256, axis=1)

    exp_own[...] = window(96 * net.own)[0:1, :96]
    for k in range(4):
        w = window(D * k + 24 * net.own)
        vectors[k][...] = w[1:2, :24]
        vectors[4 + k][...] = w[2:3, :24]
    store.wait()
    for copy in sums:
        copy.wait_send()
    finish(chains2)
    finish(chains1)


def attention_back(Z, Y, qkv, do, x, w_in, dres, p1, po, codes, lse, small):
    T, S = x.shape[0], codes.shape[0]
    cols = (tiles_of((6, 4, 5)), tiles_of((4, 2, 3)))
    blocks = (2, 2, Y, Z, 48)
    rounds = 2 + (Y == 2) + (Z - 1).bit_length()
    assert 2 ** (Z - 1).bit_length() == Z
    outs = [
        SDS((T, D), F32), SDS((24, 3 * D), F32), SDS((24, D), F32), SDS((24, FF), F32), SDS((1, 128), F32), SDS((1, 96), F32),
    ] + [SDS((1, 24), F32)] * 8
    rows = pltpu.VMEM((T, D), BF16)
    scratch = [
        pltpu.VMEM(qkv.shape, BF16), rows, pltpu.VMEM((T, 3 * D), BF16), rows, pltpu.VMEM((D, T), BF16),
        pltpu.VMEM((D, 3 * D), BF16), pltpu.VMEM((T, D), F32), pltpu.VMEM((S, LEN, LEN), F32), pltpu.VMEM((D, D), F32),
        pltpu.VMEM(blocks + (1920,), BF16), pltpu.VMEM(blocks + (1152,), BF16),
        pltpu.VMEM((rounds + 1, 8, FF), F32), pltpu.VMEM((rounds, 8, FF), F32), pltpu.VMEM((8, FF + 128), F32),
    ] + [DMA((sem_count(Z),))] * 4 + [DMA((rounds,))] * 2 + [DMA((7,)), DMA((1,))]
    scratch += scatter_scratch((Z, Y), cols[0]) + scatter_scratch((Z, Y), cols[1])
    return pl.pallas_call(
        functools.partial(attend_back_kernel, Z, Y, cols),
        out_shape=outs,
        in_specs=[ANY] * 7 + [VMEM] * 3,
        out_specs=[ANY] + [VMEM] * 13,
        scratch_shapes=scratch,
        compiler_params=pltpu.CompilerParams(collective_id=2, has_side_effects=True, vmem_limit_bytes=VMEM_LIMIT),
        name="attend_back",
    )(qkv, do, x, w_in, dres, p1, po, codes, lse, small)


def per_device(
    Z, Y, fsdp, tokens, segment_ids, valid, input_weight, query_bias, value_bias, output_weight, output_bias,
    first_gain, first_shift, expand_weight, expand_bias, shrink_weight, shrink_bias, second_gain, second_shift, cotangent,
):
    shards = (input_weight, output_weight, expand_weight, shrink_weight)
    vectors = (query_bias, value_bias, output_bias, first_gain, first_shift, expand_bias, shrink_bias, second_gain, second_shift)
    split = Y == 1 and fsdp > 1
    if split:
        def whole(v):
            return lax.all_gather(v, "fsdp", axis=0, tiled=True)

        shards, vectors = tuple(map(whole, shards)), tuple(map(whole, vectors))
    vectors = [v.reshape(1, -1) for v in vectors]
    codes = jnp.stack([segment_ids, jnp.where(valid > 0, segment_ids, -1), valid], axis=1).astype(F32)
    codes = jnp.pad(codes, ((0, 0), (0, 5), (0, 0)))
    (res, qkv, att, normed, act, gp, df, lse, w_in, w_out, w1, w2, result, dsec, vec, small) = forward(
        Z, Y, tokens, cotangent, codes, shards, vectors
    )
    p1, po, do, dres, w2_own, small = feed_back(Z, Y, act, gp, df, dsec, normed, res, att, w1, w2, w_out, vec, small)
    (dx, w_in_own, w_out_own, w1_own, stats, exp_own, *own) = attention_back(
        Z, Y, qkv, do, tokens, w_in, dres, p1, po, codes, lse, small
    )
    weights = [w_in_own, w_out_own, w1_own, w2_own]
    own = [v.reshape(-1) for v in own]
    exp_own = exp_own.reshape(-1)
    totals = stats[0, :5]
    if split:
        def share(v):
            return lax.psum_scatter(v, "fsdp", scatter_dimension=0, tiled=True)

        weights, own, exp_own = [share(v) for v in weights], [share(v) for v in own], share(exp_own)
        totals = lax.psum(totals, "fsdp")
    qb, vb, ob, fg, fs, sb, sg, ss = own
    return (
        result, dx, totals[:4] / (D * totals[4]), weights[0], qb, vb, weights[1], ob, fg, fs,
        weights[2], exp_own, weights[3], sb, sg, ss,
    )


def solution(mesh):
    dp, fsdp = mesh.shape["dp"], mesh.shape["fsdp"]
    Z, Y = dp // 4, (2 if dp * fsdp == BLOCKS else 1)
    matrix, vector = P(("dp", "fsdp"), None), P(("dp", "fsdp"))
    params = (matrix, vector, vector, matrix, vector, vector, vector, matrix, vector, matrix, vector, vector, vector)
    return jax.shard_map(
        functools.partial(per_device, Z, Y, fsdp),
        mesh=mesh,
        in_specs=(matrix, matrix, matrix) + params + (matrix,),
        out_specs=(matrix, matrix, P()) + params,
        check_vma=False,
    )
```

time: 838 us -> 313 us (0.37); the launches traced: 829 us -> 313 us
  waiting for transfers between devices: 432 us -> 0 us
  Pallas kernels: 0 us -> 296 us
  matrix products: 167 us -> 0 us
  blocking collectives: 83 us -> 0 us
  local copies, waits for them, and re-layouts: 77.8 us -> 13.5 us
  other arithmetic: 52 us -> 1.82 us
  between operations: 15.8 us -> 1.44 us
    pallas_call x0 -> x3, Pallas kernels: none -> 296 us  [the longest x1 127 us: forward(): pl.pallas_call(functools.partial(forward_kernel, Z, Y, groups), out_shape...]
    reduce_scatter x3 -> x0, waiting for transfers between devices: 283 us -> none  [the longest x1 142 us: per_device(): lax.psum_scatter(gradients[9], ('dp', 'fsdp'), scatter_dimension=0, tiled...]
    dot_general x18 -> x0, matrix products: 167 us -> none  [the longest x1 18.2 us: backward_pass(): jnp.einsum('sqhe,skhe->shqk', attended_grad, value_rows, preferred_elemen...]
    all_gather x4 -> x0, waiting for transfers between devices: 104 us -> none  [the longest x1 51.7 us: per_device(): lax.all_gather(shards[9], ('dp', 'fsdp'), axis=0, tiled=True)]
    unnamed x9 -> x0, waiting for transfers between devices: 45.2 us -> none
    unnamed x1 -> x0, blocking collectives: 42.5 us -> none
    psum x1 -> x0, blocking collectives: 40.5 us -> none  [per_device(): total_sums, total_count = lax.psum((stat_sums, local_count), ('dp', 'fsdp'))]
    unnamed x94 -> x45, local copies, waits for them, and re-layouts: 47.8 us -> 10.2 us
  transfers between devices with their start and end apart: 8 -> 0, of which waited for: 6 -> 0; matrix products, arithmetic and copies ran while one was open for 28% -> 0% of each run, Pallas kernels for 0% -> 0%
where the time goes in v2:
time: 313 us
  Pallas kernels  296 us (95%)
  local copies, waits for them, and re-layouts  13.5 us (4%)
    pallas_call x1, Pallas kernels, forward(): pl.pallas_call(functools.partial(forward_kernel, Z, Y, groups), out_shape...  127 us
    pallas_call x1, Pallas kernels, attention_back(): pl.pallas_call(functools.partial(attend_back_kernel, Z, Y, cols), out_sha...  99.3 us
    pallas_call x1, Pallas kernels, feed_back(): pl.pallas_call(functools.partial(feed_back_kernel, Z, Y, cols), out_shape...  69.5 us
    unnamed x45, local copies, waits for them, and re-layouts  10.2 us

profile of v2, /device:TPU:0, one launch (start us, length us, event | category | flops | bytes accessed | tf_op | source)
XLA Modules:
  0.0 312.8 jit_solution(18276689527127426569)
XLA Ops:
  0.6 0.7 compare_select_fusion
  1.4 0.7 stack.12
  2.1 0.7 stack.14
  2.8 0.6 pad.4.refs_2_.refs_7_
  3.4 127.2 %forward.1 = (f32[1024,768]{1,0:T(8,128)}, bf16[18,1024,128]{2,1,0:T(8,128)(2,1)}, bf16[1024,768]{1,0:T(8,128)(2,1)}, bf16[1024,768]{1,0:T(8,128)(2,1)}, bf16[10...) custom-call(bf16[1024,768]{1,0:T(8,128)(2,1)} %refs_2_.1, ...), custom_call_target="tpu_custom_call" | custom-call | tf_op jit(solution)/shard_map/forward/pallas_call | solution.py:677
  130.5 69.5 %feed_back.1 = (bf16[2,2,2,4,48,1536]{5,4,3,2,1,0:T(8,128)(2,1)}, bf16[2,2,2,4,48,384]{5,4,3,2,1,0:T(8,128)(2,1)}, bf16[1024,768]{1,0:T(8,128)(2,1)}, f32[1024,7...) custom-call(bf16[1024,3072]{1,0:T(8,128)(2,1)} %get-tuple-element.54.refs_0_, ...), custom_call_target="tpu_custom_call" | custom-call | tf_op jit(solution)/shard_map/feed_back/pallas_call | solution.py:843
  200.0 0.0 copy-start.1
  200.0 99.3 %attend_back.1 = (f32[1024,768]{1,0:T(8,128)}, f32[24,2304]{1,0:T(8,128)}, f32[24,768]{1,0:T(8,128)}, f32[24,3072]{1,0:T(8,128)}, f32[1,128]{1,0:T(1,128)}, /*in...) custom-call(bf16[18,1024,128]{2,1,0:T(8,128)(2,1)} %get-tuple-elemen, ...), custom_call_target="tpu_custom_call" | custom-call | tf_op jit(solution)/shard_map/attend_back/pallas_call | solution.py:1031
  299.4 0.0 copy-start
  299.4 1.3 slice.12
  301.4 1.1 divide_bitcast_fusion
  302.5 1.1 copy.48
  303.7 1.7 copy.49
  305.4 0.7 copy.50
  306.1 0.5 copy.51
  306.6 0.0 copy-done.13
  306.6 0.5 copy.52
  307.1 0.0 copy-done.5
  307.1 0.6 copy.53
  307.7 0.5 copy.54
  308.2 0.5 copy.55
  308.8 0.0 copy-done.10
  308.8 0.5 copy.56
  309.3 0.0 copy-done.3
  309.3 0.7 copy.57
  310.0 0.0 copy-done.9
  310.0 0.5 copy.58
  310.5 0.7 copy.59
  311.2 0.0 copy-done.8
  311.2 0.5 copy.60
  311.7 0.5 copy.61
  312.3 0.5 copy.62
  (24 shorter events, 0.1 us)
Async XLA Ops:
  200.0 102.4 %copy-start.1 = (bf16[1024,768]{1,0:T(8,128)(2,1)S(1)}, bf16[1024,768]{1,0:T(8,128)(2,1)}, u32[]{:S(2)}) copy-start(bf16[1024,768]{1,0:T(8,128)(2,1)} %get-tuple-element.104) | copy-start | bytes 4718596
  299.4 4.2 %copy-start = (f32[1024,768]{1,0:T(8,128)S(1)}, f32[1024,768]{1,0:T(8,128)}, u32[]{:S(2)}) copy-start(f32[1024,768]{1,0:T(8,128)} %get-tuple-element.105) | copy-start | bytes 9437188
  303.6 1.8 copy-start.4
  303.6 2.5 copy-start.14
  303.6 3.0 copy-start.13
  303.6 3.5 %copy-start.5 = (f32[24,768]{1,0:T(8,128)S(1)}, f32[24,768]{1,0:T(8,128)}, u32[]{:S(2)}) copy-start(f32[24,768]{1,0:T(8,128)} %get-tuple-element.110) | copy-start | bytes 221188
  303.6 4.1 %copy-start.12 = (f32[1,24]{1,0:T(1,128)S(1)}, f32[1,24]{1,0:T(1,128)}, u32[]{:S(2)}) copy-start(f32[1,24]{1,0:T(1,128)} %get-tuple-element.79) | copy-start | bytes 292
  303.6 4.6 %copy-start.11 = (f32[1,24]{1,0:T(1,128)S(1)}, f32[1,24]{1,0:T(1,128)}, u32[]{:S(2)}) copy-start(f32[1,24]{1,0:T(1,128)} %get-tuple-element.80) | copy-start | bytes 292
  303.6 5.1 %copy-start.10 = (f32[1,24]{1,0:T(1,128)S(1)}, f32[1,24]{1,0:T(1,128)}, u32[]{:S(2)}) copy-start(f32[1,24]{1,0:T(1,128)} %get-tuple-element.81) | copy-start | bytes 292
  303.6 5.6 %copy-start.3 = (f32[24,3072]{1,0:T(8,128)S(1)}, f32[24,3072]{1,0:T(8,128)}, u32[]{:S(2)}) copy-start(f32[24,3072]{1,0:T(8,128)} %get-tuple-element.114) | copy-start | bytes 884740
  303.7 6.3 %copy-start.9 = (f32[1,96]{1,0:T(1,128)S(1)}, f32[1,96]{1,0:T(1,128)}, u32[]{:S(2)}) copy-start(f32[1,96]{1,0:T(1,128)} %get-tuple-element.83) | copy-start | bytes 1156
  303.7 6.8 %copy-start.2 = (f32[96,768]{1,0:T(8,128)S(1)}, f32[96,768]{1,0:T(8,128)}, u32[]{:S(2)}) copy-start(f32[96,768]{1,0:T(8,128)} %get-tuple-element.116) | copy-start | bytes 884740
  303.7 7.5 %copy-start.8 = (f32[1,24]{1,0:T(1,128)S(1)}, f32[1,24]{1,0:T(1,128)}, u32[]{:S(2)}) copy-start(f32[1,24]{1,0:T(1,128)} %get-tuple-element.85) | copy-start | bytes 292
  303.7 8.1 %copy-start.7 = (f32[1,24]{1,0:T(1,128)S(1)}, f32[1,24]{1,0:T(1,128)}, u32[]{:S(2)}) copy-start(f32[1,24]{1,0:T(1,128)} %get-tuple-element.86) | copy-start | bytes 292
  303.7 8.6 %copy-start.6 = (f32[1,24]{1,0:T(1,128)S(1)}, f32[1,24]{1,0:T(1,128)}, u32[]{:S(2)}) copy-start(f32[1,24]{1,0:T(1,128)} %get-tuple-element.87) | copy-start | bytes 292
